TPU v7x, 768 devices: a whole 4x8x12 slice. The times are simulated.
768 devices in a mesh: tile: 96 (over z, x, core), rep: 8 (over y).
Axes of the slice: x: 4, y: 8, z: 12, core: 2. Of those that a mesh axis runs over, the one named last changes fastest.
Arguments:
- amps: bfloat16 [768, 8, 1920], P('tile', 'rep'), may hold values from -6 to 6
- cycle_w: bfloat16 [8, 1920, 98304], P('rep', None, 'tile'), may hold values from -0.125 to 0.125
- occ_irrep: int32 [8], P('rep'), may hold values from 0 to 7
- vir_irrep: int32 [1920], replicated, may hold values from 0 to 7
- col_irrep: int32 [98304], P('tile'), may hold values from 0 to 7
Outputs:
- residual: bfloat16 [768, 98304], P('rep', 'tile')
All inputs are finite; a program needn't handle non-finite values.
Results may differ from a plain program's by a relative error of at most 0.017.
Values may be sent and summed in bfloat16 or wider, within the bound.
No kernel may reach another device: no remote copies, remote signals or barrier semaphores. Data moves between devices by JAX's collectives and lax.ppermute only.
A program may use at most 32 MiB of HBM per device.

v0:
```python
import jax
import jax.numpy as jnp
from jax import lax
from jax.sharding import PartitionSpec as P


def on_device(amps, cycle_w, occ_irrep, vir_irrep, col_irrep):
    row_count, k_count, v_count = amps.shape
    pair_sym = jnp.bitwise_xor(occ_irrep[:, None], vir_irrep[None, :]).reshape(-1)
    allowed = pair_sym[:, None] == col_irrep[None, :]
    weights = cycle_w.reshape(k_count * v_count, cycle_w.shape[2])
    masked = jnp.where(allowed, weights, jnp.zeros((), weights.dtype))
    flat_amps = amps.reshape(row_count, k_count * v_count)
    panel = lax.all_gather(flat_amps, "tile", axis=0, tiled=True)
    terms = jnp.dot(panel, masked, preferred_element_type=jnp.float32)
    summed = lax.psum_scatter(terms.astype(jnp.bfloat16), "rep", scatter_dimension=0, tiled=True)
    return summed


def solution(mesh):
    in_specs = (P("tile", "rep", None), P("rep", None, "tile"), P("rep"), P(), P("tile"))
    out_specs = P("rep", "tile")
    return jax.shard_map(
        on_device, mesh=mesh, in_specs=in_specs, out_specs=out_specs, check_vma=False
    )
```

profile of v0, /device:TPU:6, one launch (start us, length us, event | category | flops | bytes accessed | tf_op | source)
XLA Modules:
  0.0 191.9 jit_solution(15906706358509480767)
XLA Ops:
  6.5 0.0 all-gather.3.cloned.1.call-start
  6.5 0.7 all-gather.3.cloned.1.call-update
  7.3 0.0 reduce-scatter.4.cloned.1.call-start
  7.9 0.7 broadcast_xor_fusion
  8.6 125.3 %all-gather.3.cloned.1.call-done = bf16[768,1,1920]{2,0,1:T(8,128)(2,1)} async-done(((bf16[8,1,1920]{2,0,1:T(8,128)(2,1)}), bf16[768,1,1920]{2,0,1:T(8,128)(2,1)}) %all-gather.3.cloned.1.call-update) | async-done | bytes 2949136 | tf_op jit(solution)/shard_map/all_gather | solution.py:14
  133.9 6.9 %fusion.9 = bf16[768,1024]{0,1:T(8,128)(2,1)S(1)} fusion(bf16[768,1,1920]{2,0,1:T(8,128)(2,1)} %all-gather.3.cloned.1.call-done, bf16[1,1920,1024]{2,1,0:T(8,128)(2,1)} %param.6, s32[1024]{0:T(1024)} %param.9, s32[1920]{0:T(1024)S(1)} %broadcast_xor_fusion), kind=kOutput, calls=%fused_computation.8 | convolution fusion | flops 3024617472 | bytes 8465920 | tf_op jit(solution)/shard_map/dot_general | solution.py:15
  140.8 1.6 copy.8
  142.5 0.0 reduce-scatter.4.cloned.1.call-update
  142.5 42.6 %reduce-scatter.4.cloned.1.call-done = bf16[96,1024]{1,0:T(8,128)(2,1)} async-done(((bf16[768,1024]{1,0:T(8,128)(2,1)}), bf16[96,1024]{1,0:T(8,128)(2,1)}) %reduce-scatter.4.cloned.1.call-update) | async-done | bytes 196624 | tf_op jit(solution)/shard_map/reduce_scatter | solution.py:16
Async XLA Ops:
  6.5 127.4 %all-gather.3.cloned.1.call-start = ((), (), s32[]{:S(2)}) async-start(), calls=%async_computation.1 | async-start | bytes 2979840 | tf_op jit(solution)/shard_map/all_gather | solution.py:14
  7.3 177.9 %reduce-scatter.4.cloned.1.call-start = ((), (), s32[]{:S(2)}) async-start(), calls=%async_computation.2 | async-start | bytes 1769472 | tf_op jit(solution)/shard_map/reduce_scatter | solution.py:16
Sparse Core Ops, SparseCore 0:
  11.0 122.8 all-gather.2
  142.6 42.4 reduce-scatter.3
where the time goes:
time: 192 us
  waiting for transfers between devices  169 us (88%)
  between operations  14.1 us (7%)
  matrix products  6.86 us (4%)
    all_gather x1, waiting for transfers between devices, on_device(): panel = lax.all_gather(flat_amps, 'tile', axis=0, tiled=True)  125 us
    reduce_scatter x1, waiting for transfers between devices, on_device(): lax.psum_scatter(terms.astype(jnp.bfloat16), 'rep', scatter_dimension=0,...  42.6 us
    dot_general x1, matrix products, on_device(): terms = jnp.dot(panel, masked, preferred_element_type=jnp.float32)  6.86 us
  transfers between devices with their start and end apart: 2, of which 2 were waited for; matrix products, arithmetic and copies ran while one was open for 0% of the time, Pallas kernels for 0%

commit v1 on v0

v1 whole, which is shorter than its diff:
```python
import jax
import jax.numpy as jnp
from jax import lax
from jax.sharding import Mesh, PartitionSpec as P

NZ, NX, NC, NY = 12, 4, 2, 8
F32 = jnp.float32
BF16 = jnp.bfloat16


def shift(array, axis, size, step):
    return lax.ppermute(array, axis, [(i, (i + step) % size) for i in range(size)])


def gather(block, axis, size):
    copies = jnp.broadcast_to(block[None], (size,) + block.shape)
    return lax.all_to_all(copies, axis, 0, 0, tiled=False)


def reduce_scatter(terms):
    y = lax.axis_index("y")
    rows = terms.shape[0] // NY
    half = terms.shape[1] // 2

    def chunk(d):
        return lax.dynamic_slice_in_dim(terms, ((d + NY) % NY) * rows, rows)

    far = chunk(y + 4)
    from_right = shift(jnp.concatenate([chunk(y - 3), chunk(y - 1)], 0), "y", NY, -1)
    from_left = shift(jnp.concatenate([chunk(y + 3), chunk(y + 1)], 0), "y", NY, 1)
    far_right = shift(far[:, :half], "y", NY, -2)
    far_left = shift(far[:, half:], "y", NY, 2)
    down = chunk(y - 2).astype(F32) + from_right[:rows].astype(F32)
    down = jnp.concatenate([down[:, :half] + far_right.astype(F32), down[:, half:]], 1).astype(BF16)
    up = chunk(y + 2).astype(F32) + from_left[:rows].astype(F32)
    up = jnp.concatenate([up[:, :half], up[:, half:] + far_left.astype(F32)], 1).astype(BF16)
    got_down = shift(down, "y", NY, -2)
    got_up = shift(up, "y", NY, 2)
    total = chunk(y).astype(F32) + from_right[rows:].astype(F32) + from_left[rows:].astype(F32)
    return (total + got_down.astype(F32) + got_up.astype(F32)).astype(BF16)


def on_device(amps, cycle_w, occ_irrep, vir_irrep, col_irrep):
    c = lax.axis_index("c")
    pair_sym = jnp.bitwise_xor(occ_irrep[:, None], vir_irrep[None, :]).reshape(-1)
    allowed = pair_sym[:, None] == col_irrep[None, :]
    weights = cycle_w.reshape(-1, cycle_w.shape[2])
    masked = lax.optimization_barrier(jnp.where(allowed, weights, jnp.zeros((), weights.dtype)))
    block = amps.reshape(amps.shape[0], -1)
    along_z = gather(block, "z", NZ)
    mine = gather(along_z, "x", NX).reshape(-1, block.shape[1])
    theirs = shift(mine, "c", NC, 1)

    def product(rows):
        return jnp.dot(rows, masked, preferred_element_type=F32).astype(BF16)

    here = product(mine).reshape(NX, NZ, amps.shape[0], -1)
    there = product(theirs).reshape(NX, NZ, amps.shape[0], -1)
    first = jnp.where(c == 0, here, there)
    second = jnp.where(c == 0, there, here)
    terms = jnp.stack([first, second], 2).transpose(1, 0, 2, 3, 4).reshape(-1, here.shape[-1])
    return reduce_scatter(terms)


def solution(mesh):
    fine = Mesh(mesh.devices.reshape(NZ, NX, NC, NY), ("z", "x", "c", "y"))
    tile = ("z", "x", "c")
    in_specs = (P(tile, "y", None), P("y", None, tile), P("y"), P(), P(tile))
    return jax.shard_map(
        on_device, mesh=fine, in_specs=in_specs, out_specs=P("y", tile), check_vma=False
    )
```

time: 192 us -> 112 us (0.58)
  the two profiles are of different devices: /device:TPU:6 before, /device:TPU:88 now
where the time goes in v1:
time: 112 us
  blocking collectives  57.5 us (51%)
  starting transfers between devices  23.2 us (21%)
  waiting for transfers between devices  17.4 us (16%)
  matrix products  5.91 us (5%)
  other arithmetic  5.27 us (5%)
  local copies, waits for them, and re-layouts  1.17 us (1%)
    all_to_all x2, blocking collectives, gather(): return lax.all_to_all(copies, axis, 0, 0, tiled=False)  57.5 us
    ppermute x7, starting transfers between devices, shift(): lax.ppermute(array, axis, [(i, (i + step) % size) for i in range(size)])  23.2 us
    ppermute x7, waiting for transfers between devices, shift(): lax.ppermute(array, axis, [(i, (i + step) % size) for i in range(size)])  17.4 us
    dot_general x2, matrix products, product(): return jnp.dot(rows, masked, preferred_element_type=F32).astype(BF16)  5.91 us
    select_n x1, other arithmetic, on_device(): jnp.where(allowed, weights, jnp.zeros((), weights.dtype))  4.05 us
  transfers between devices with their start and end apart: 7, of which 3 were waited for; matrix products, arithmetic and copies ran while one was open for 8% of the time, Pallas kernels for 0%

profile of v1, /device:TPU:88, one launch (start us, length us, event | category | flops | bytes accessed | tf_op | source)
XLA Modules:
  0.0 111.5 jit_solution(17193010513838271253)
XLA Ops:
  0.0 0.8 broadcast_in_dim.22
  0.8 33.6 %all_to_all.10 = bf16[12,8,1920]{2,1,0:T(8,128)(2,1)S(1)} all-to-all(bf16[12,8,1920]{2,1,0:T(8,128)(2,1)S(1)} %broadcast_in_dim.22), channel_id=1, replica_groups=mesh['z'=12,'x'=4,'c'=2,'y'=8] {'z'}, dimensions={0} | all-to-all | bytes 737280 | tf_op jit(solution)/shard_map/all_to_all | solution.py:17
  34.4 0.1 broadcast_in_dim.23
  34.5 0.0 copy-start.1
  34.5 0.0 copy-start.2
  34.5 23.9 %all_to_all.11 = bf16[4,12,8,1920]{3,2,1,0:T(8,128)(2,1)S(1)} all-to-all(bf16[4,12,8,1920]{3,2,1,0:T(8,128)(2,1)S(1)} %broadcast_in_dim.23), channel_id=1, replica_groups=mesh['z'=12,'x'=4,'c'=2,'y'=8] {'x'}, dimensions={0} | all-to-all | bytes 2949120 | tf_op jit(solution)/shard_map/all_to_all | solution.py:17
  58.4 1.9 %collective-permute-start = (bf16[384,1920]{1,0:T(8,128)(2,1)S(1)}, bf16[384,1920]{1,0:T(8,128)(2,1)S(1)}, u32[]{:S(2)}, u32[]{:S(2)}) collective-permute-start(bf16[384,1920]{1,0:T(8,128)(2,1)S(1)} %bitcast.23), channel_id=1, source_target_pairs={{0,8},{8,0},{1,9},{9,1},{2,10},{10,2},{3,11},{11,3},{4,12},{12,4},... | collective-permute-start | bytes 4423688 | tf_op jit(solution)/shard_map/ppermute | solution.py:12
  61.0 0.0 copy-done.1
  61.1 0.0 copy-done.2
  61.1 4.1 %compare_select_fusion = bf16[1920,1024]{1,0:T(8,128)(2,1)} fusion(bf16[1,1920,1024]{2,1,0:T(8,128)(2,1)} %param.6, s32[1024]{0:T(1024)S(1)} %copy-done.2, s32[1920]{0:T(1024)S(1)} %broadcast_xor_fusion), kind=kLoop, calls=%fused_computation | loop fusion | flops 3932160 | bytes 7876096 | tf_op jit(solution)/shard_map/jit(_where)/select_n | solution.py:48
  65.1 0.0 copy-start
  65.1 4.0 %convolution_convert_fusion.1 = bf16[1024,384]{0,1:T(8,128)(2,1)S(1)} fusion(bf16[384,1920]{1,0:T(8,128)(2,1)S(1)} %bitcast.24, bf16[1920,1024]{1,0:T(8,128)(2,1)} %compare_select_fusion), kind=kOutput, calls=%fused_computation.3 | convolution fusion | flops 1510342656 | bytes 6193152 | tf_op jit(solution)/shard_map/dot_general | solution.py:55
  69.2 0.0 collective-permute-done
  69.2 0.0 copy-done
  69.2 1.9 %broadcast_select_fusion.1 = (bf16[1024,384]{0,1:T(8,128)(2,1)S(1)}, bf16[1024,384]{0,1:T(8,128)(2,1)S(1)}) fusion(bf16[1024,384]{0,1:T(8,128)(2,1)S(1)} %convolution_convert_fusion.1, pred[]{:T(512)S(6)} %eq.26, bf16[384,1920]{1,0:T(8,128)(2,1)S(1)} %collective-permute-done, bf16[1920,1024]{1,0:T(8,128)(2,1)S(1)} %copy-done), kind=kOutput, calls=%fused_computation.5 | convolution fusion | flops 1511129088 | bytes 7766017 | tf_op jit(solution)/shard_map/dot_general | solution.py:55
  71.1 0.1 maximum_bitcast_fusion
  71.2 0.2 copy.6
  71.4 0.1 constant_dynamic-slice_fusion.4
  71.5 4.7 %collective-permute-start.2 = (bf16[192,1024]{1,0:T(8,128)(2,1)S(1)}, bf16[192,1024]{1,0:T(8,128)(2,1)S(1)}, u32[]{:S(2)}, u32[]{:S(2)}) collective-permute-start(bf16[192,1024]{1,0:T(8,128)(2,1)S(1)} %pad_maximum_fusion.1), channel_id=1, source_target_pairs={{0,1},{1,2},{2,3},{3,4},{4,5},{5,6},{6,7},{7,0},{8,9},{9,10},{10,1... | collective-permute-start | bytes 1179656 | tf_op jit(solution)/shard_map/ppermute | solution.py:12
  76.3 1.9 %collective-permute-start.1 = (bf16[192,1024]{1,0:T(8,128)(2,1)S(1)}, bf16[192,1024]{1,0:T(8,128)(2,1)S(1)}, u32[]{:S(2)}, u32[]{:S(2)}) collective-permute-start(bf16[192,1024]{1,0:T(8,128)(2,1)S(1)} %pad_maximum_fusion), channel_id=1, source_target_pairs={{0,7},{1,0},{2,1},{3,2},{4,3},{5,4},{6,5},{7,6},{8,15},{9,8},{10,9... | collective-permute-start | bytes 1179656 | tf_op jit(solution)/shard_map/ppermute | solution.py:12
  78.3 1.9 %collective-permute-start.3 = (bf16[96,512]{1,0:T(8,128)(2,1)S(1)}, bf16[96,512]{1,0:T(8,128)(2,1)S(1)}, u32[]{:S(2)}, u32[]{:S(2)}) collective-permute-start(bf16[96,512]{1,0:T(8,128)(2,1)S(1)} %get-tuple-element.5), channel_id=1, source_target_pairs={{0,6},{1,7},{2,0},{3,1},{4,2},{5,3},{6,4},{7,5},{8,14},{9,15},{10,... | collective-permute-start | bytes 294920 | tf_op jit(solution)/shard_map/ppermute | solution.py:12
  80.2 6.0 %collective-permute-start.5 = (bf16[96,512]{1,0:T(8,128)(2,1)S(1)}, bf16[96,512]{1,0:T(8,128)(2,1)S(1)}, u32[]{:S(2)}, u32[]{:S(2)}) collective-permute-start(bf16[96,512]{1,0:T(8,128)(2,1)S(1)} %get-tuple-element.6), channel_id=1, source_target_pairs={{0,2},{1,3},{2,4},{3,5},{4,6},{5,7},{6,0},{7,1},{8,10},{9,11},{10,... | collective-permute-start | bytes 294920 | tf_op jit(solution)/shard_map/ppermute | solution.py:12
  86.2 0.0 collective-permute-done.2
  86.2 7.2 %collective-permute-done.1 = bf16[192,1024]{1,0:T(8,128)(2,1)S(1)} collective-permute-done((bf16[192,1024]{1,0:T(8,128)(2,1)S(1)}, bf16[192,1024]{1,0:T(8,128)(2,1)S(1)}, u32[]{:S(2)}, u32[]{:S(2)}) %collective-permute-start.1) | collective-permute-done | bytes 393248 | tf_op jit(solution)/shard_map/ppermute | solution.py:12
  93.4 0.1 convert_add_fusion.1
  93.6 0.0 collective-permute-done.5
  93.6 3.4 %collective-permute-start.6 = (bf16[96,1024]{1,0:T(8,128)(2,1)S(1)}, bf16[96,1024]{1,0:T(8,128)(2,1)S(1)}, u32[]{:S(2)}, u32[]{:S(2)}) collective-permute-start(bf16[96,1024]{1,0:T(8,128)(2,1)S(1)} %pad_maximum_fusion.3), channel_id=1, source_target_pairs={{0,2},{1,3},{2,4},{3,5},{4,6},{5,7},{6,0},{7,1},{8,10},{9,11},{10,... | collective-permute-start | bytes 589832 | tf_op jit(solution)/shard_map/ppermute | solution.py:12
  97.0 0.0 collective-permute-done.3
  97.1 3.4 %collective-permute-start.4 = (bf16[96,1024]{1,0:T(8,128)(2,1)S(1)}, bf16[96,1024]{1,0:T(8,128)(2,1)S(1)}, u32[]{:S(2)}, u32[]{:S(2)}) collective-permute-start(bf16[96,1024]{1,0:T(8,128)(2,1)S(1)} %pad_maximum_fusion.2), channel_id=1, source_target_pairs={{0,6},{1,7},{2,0},{3,1},{4,2},{5,3},{6,4},{7,5},{8,14},{9,15},{10,... | collective-permute-start | bytes 589832 | tf_op jit(solution)/shard_map/ppermute | solution.py:12
  100.5 4.0 %collective-permute-done.6 = bf16[96,1024]{1,0:T(8,128)(2,1)S(1)} collective-permute-done((bf16[96,1024]{1,0:T(8,128)(2,1)S(1)}, bf16[96,1024]{1,0:T(8,128)(2,1)S(1)}, u32[]{:S(2)}, u32[]{:S(2)}) %collective-permute-start.6) | collective-permute-done | bytes 196640 | tf_op jit(solution)/shard_map/ppermute | solution.py:12
  104.4 6.3 %collective-permute-done.4 = bf16[96,1024]{1,0:T(8,128)(2,1)S(1)} collective-permute-done((bf16[96,1024]{1,0:T(8,128)(2,1)S(1)}, bf16[96,1024]{1,0:T(8,128)(2,1)S(1)}, u32[]{:S(2)}, u32[]{:S(2)}) %collective-permute-start.4) | collective-permute-done | bytes 196640 | tf_op jit(solution)/shard_map/ppermute | solution.py:12
  110.7 0.8 add_convert_fusion
  (10 shorter events, 0.2 us)
Async XLA Ops:
  34.5 26.5 %copy-start.1 = (s32[1920]{0:T(1024)S(1)}, s32[1920]{0:T(1024)}, u32[]{:S(2)}) copy-start(s32[1920]{0:T(1024)} %param.8) | copy-start | bytes 23044
  34.5 26.5 %copy-start.2 = (s32[1024]{0:T(1024)S(1)}, s32[1024]{0:T(1024)}, u32[]{:S(2)}) copy-start(s32[1024]{0:T(1024)} %param.9) | copy-start | bytes 12292
  58.4 10.8 %collective-permute-start = (bf16[384,1920]{1,0:T(8,128)(2,1)S(1)}, bf16[384,1920]{1,0:T(8,128)(2,1)S(1)}, u32[]{:S(2)}, u32[]{:S(2)}) collective-permute-start(bf16[384,1920]{1,0:T(8,128)(2,1)S(1)} %bitcast.23), channel_id=1, source_target_pairs={{0,8},{8,0},{1,9},{9,1},{2,10},{10,2},{3,11},{11,3},{4,12},{12,4},... | collective-permute-start | bytes 4423688 | tf_op jit(solution)/shard_map/ppermute | solution.py:12
  65.1 4.1 %copy-start = (bf16[1920,1024]{1,0:T(8,128)(2,1)S(1)}, bf16[1920,1024]{1,0:T(8,128)(2,1)}, u32[]{:S(2)}) copy-start(bf16[1920,1024]{1,0:T(8,128)(2,1)} %compare_select_fusion) | copy-start | bytes 11796484
  71.5 14.7 %collective-permute-start.2 = (bf16[192,1024]{1,0:T(8,128)(2,1)S(1)}, bf16[192,1024]{1,0:T(8,128)(2,1)S(1)}, u32[]{:S(2)}, u32[]{:S(2)}) collective-permute-start(bf16[192,1024]{1,0:T(8,128)(2,1)S(1)} %pad_maximum_fusion.1), channel_id=1, source_target_pairs={{0,1},{1,2},{2,3},{3,4},{4,5},{5,6},{6,7},{7,0},{8,9},{9,10},{10,1... | collective-permute-start | bytes 1179656 | tf_op jit(solution)/shard_map/ppermute | solution.py:12
  76.3 17.2 %collective-permute-start.1 = (bf16[192,1024]{1,0:T(8,128)(2,1)S(1)}, bf16[192,1024]{1,0:T(8,128)(2,1)S(1)}, u32[]{:S(2)}, u32[]{:S(2)}) collective-permute-start(bf16[192,1024]{1,0:T(8,128)(2,1)S(1)} %pad_maximum_fusion), channel_id=1, source_target_pairs={{0,7},{1,0},{2,1},{3,2},{4,3},{5,4},{6,5},{7,6},{8,15},{9,8},{10,9... | collective-permute-start | bytes 1179656 | tf_op jit(solution)/shard_map/ppermute | solution.py:12
  78.3 18.8 %collective-permute-start.3 = (bf16[96,512]{1,0:T(8,128)(2,1)S(1)}, bf16[96,512]{1,0:T(8,128)(2,1)S(1)}, u32[]{:S(2)}, u32[]{:S(2)}) collective-permute-start(bf16[96,512]{1,0:T(8,128)(2,1)S(1)} %get-tuple-element.5), channel_id=1, source_target_pairs={{0,6},{1,7},{2,0},{3,1},{4,2},{5,3},{6,4},{7,5},{8,14},{9,15},{10,... | collective-permute-start | bytes 294920 | tf_op jit(solution)/shard_map/ppermute | solution.py:12
  80.2 13.4 %collective-permute-start.5 = (bf16[96,512]{1,0:T(8,128)(2,1)S(1)}, bf16[96,512]{1,0:T(8,128)(2,1)S(1)}, u32[]{:S(2)}, u32[]{:S(2)}) collective-permute-start(bf16[96,512]{1,0:T(8,128)(2,1)S(1)} %get-tuple-element.6), channel_id=1, source_target_pairs={{0,2},{1,3},{2,4},{3,5},{4,6},{5,7},{6,0},{7,1},{8,10},{9,11},{10,... | collective-permute-start | bytes 294920 | tf_op jit(solution)/shard_map/ppermute | solution.py:12
  93.6 10.8 %collective-permute-start.6 = (bf16[96,1024]{1,0:T(8,128)(2,1)S(1)}, bf16[96,1024]{1,0:T(8,128)(2,1)S(1)}, u32[]{:S(2)}, u32[]{:S(2)}) collective-permute-start(bf16[96,1024]{1,0:T(8,128)(2,1)S(1)} %pad_maximum_fusion.3), channel_id=1, source_target_pairs={{0,2},{1,3},{2,4},{3,5},{4,6},{5,7},{6,0},{7,1},{8,10},{9,11},{10,... | collective-permute-start | bytes 589832 | tf_op jit(solution)/shard_map/ppermute | solution.py:12
  97.1 13.6 %collective-permute-start.4 = (bf16[96,1024]{1,0:T(8,128)(2,1)S(1)}, bf16[96,1024]{1,0:T(8,128)(2,1)S(1)}, u32[]{:S(2)}, u32[]{:S(2)}) collective-permute-start(bf16[96,1024]{1,0:T(8,128)(2,1)S(1)} %pad_maximum_fusion.2), channel_id=1, source_target_pairs={{0,6},{1,7},{2,0},{3,1},{4,2},{5,3},{6,4},{7,5},{8,14},{9,15},{10,... | collective-permute-start | bytes 589832 | tf_op jit(solution)/shard_map/ppermute | solution.py:12

commit v2 on v0

v2 whole, which is shorter than its diff:
```python
import jax
import jax.numpy as jnp
from jax import lax
from jax.sharding import Mesh, PartitionSpec as P

ZH, ZL, NX, NC, NY = 6, 2, 4, 2, 8
F32 = jnp.float32
BF16 = jnp.bfloat16
tie = lax.optimization_barrier


def gather(block, axis, size):
    copies = jnp.broadcast_to(block[None], (size,) + block.shape)
    return lax.all_to_all(copies, axis, 0, 0, tiled=False)


def mirrored(array, step):
    pairs = []
    for c in range(NC):
        for y in range(NY):
            to = (y + (step if c == 0 else -step)) % NY
            pairs.append((c * NY + y, c * NY + to))
    return lax.ppermute(array, ("c", "y"), pairs)


def plus(*terms):
    total = terms[0].astype(F32)
    for term in terms[1:]:
        total = total + term.astype(F32)
    return total.astype(BF16)


def reduce_scatter(terms):
    y = lax.axis_index("y")
    sign = 1 - 2 * lax.axis_index("c")

    def part(offset):
        return lax.dynamic_index_in_dim(terms, (y + sign * offset + NY) % NY, 0, keepdims=False)

    near_down = mirrored(jnp.stack([part(-1), part(-3)]), -1)
    near_up = mirrored(jnp.stack([part(1), part(3)]), 1)
    far = mirrored(part(4), 2)
    down = plus(part(-2), near_down[1])
    got_down = mirrored(down, -2)
    up = plus(part(2), near_up[1], far)
    got_up = mirrored(up, 2)
    return plus(part(0), near_down[0], near_up[0], got_down, got_up)


def on_device(amps, cycle_w, occ_irrep, vir_irrep, col_irrep):
    c = lax.axis_index("c")
    pair_sym = jnp.bitwise_xor(occ_irrep[:, None], vir_irrep[None, :]).reshape(-1)
    allowed = pair_sym.astype(BF16)[:, None] == col_irrep.astype(BF16)[None, :]
    weights = cycle_w.reshape(-1, cycle_w.shape[2])
    block = amps.reshape(amps.shape[0], -1)
    along_z = gather(block, "zh", ZH)
    mine = gather(along_z, ("zl", "x"), ZL * NX)
    theirs = lax.ppermute(mine, "c", [(0, 1), (1, 0)])
    masked = tie(jnp.where(allowed, weights, jnp.zeros((), weights.dtype)))

    def product(rows):
        part = jnp.dot(rows.reshape(-1, rows.shape[-1]), masked, preferred_element_type=F32).astype(BF16)
        return part.reshape(ZL, NX, ZH, -1, part.shape[-1]).transpose(2, 0, 1, 3, 4)

    here = product(mine)
    there = product(theirs)
    first = jnp.where(c == 0, here, there)
    second = jnp.where(c == 0, there, here)
    terms = jnp.stack([first, second], 3).reshape(NY, -1, weights.shape[1])
    return reduce_scatter(terms)


def solution(mesh):
    fine = Mesh(mesh.devices.reshape(ZH, ZL, NX, NC, NY), ("zh", "zl", "x", "c", "y"))
    tile = ("zh", "zl", "x", "c")
    in_specs = (P(tile, "y", None), P("y", None, tile), P("y"), P(), P(tile))
    return jax.shard_map(
        on_device, mesh=fine, in_specs=in_specs, out_specs=P("y", tile), check_vma=False
    )
```

time: 192 us -> 101 us (0.53)
  the two profiles are of different devices: /device:TPU:6 before, /device:TPU:1 now
where the time goes in v2:
time: 101 us; the launch traced here: 100 us
  blocking collectives  46.6 us (46%)
  starting transfers between devices  26 us (26%)
  waiting for transfers between devices  14.1 us (14%)
  matrix products  5.91 us (6%)
  other arithmetic  5.55 us (5%)
  local copies, waits for them, and re-layouts  1.13 us (1%)
    all_to_all x2, blocking collectives, gather(): return lax.all_to_all(copies, axis, 0, 0, tiled=False)  46.6 us
    ppermute x5, starting transfers between devices, mirrored(): return lax.ppermute(array, ('c', 'y'), pairs)  19 us
    ppermute x5, waiting for transfers between devices, mirrored(): return lax.ppermute(array, ('c', 'y'), pairs)  14.1 us
    ppermute x1, starting transfers between devices, on_device(): theirs = lax.ppermute(mine, 'c', [(0, 1), (1, 0)])  6.96 us
    dot_general x2, matrix products, product(): jnp.dot(rows.reshape(-1, rows.shape[-1]), masked, preferred_element_type=...  5.91 us
    select_n x1, other arithmetic, on_device(): masked = tie(jnp.where(allowed, weights, jnp.zeros((), weights.dtype)))  4.35 us
  transfers between devices with their start and end apart: 6, of which 3 were waited for; matrix products, arithmetic and copies ran while one was open for 9% of the time, Pallas kernels for 0%

profile of v2, /device:TPU:1, one launch (start us, length us, event | category | flops | bytes accessed | tf_op | source)
XLA Modules:
  0.0 100.2 jit_solution(14244106126108888192)
XLA Ops:
  0.0 0.8 broadcast_in_dim.11
  0.8 24.6 %all_to_all.10 = bf16[6,8,1920]{2,1,0:T(8,128)(2,1)S(1)} all-to-all(bf16[6,8,1920]{2,1,0:T(8,128)(2,1)S(1)} %broadcast_in_dim.11), channel_id=1, replica_groups=mesh['zh'=6,'zl'=2,'x'=4,'c'=2,'y'=8] {'zh'}, dimensions={0} | all-to-all | bytes 368640 | tf_op jit(solution)/shard_map/all_to_all | solution.py:14
  25.3 0.1 broadcast_in_dim.24
  25.4 0.0 copy-start.2
  25.4 0.0 copy-start.1
  25.5 22.0 %all_to_all.11 = bf16[8,6,8,1920]{3,2,1,0:T(8,128)(2,1)S(1)} all-to-all(bf16[8,6,8,1920]{3,2,1,0:T(8,128)(2,1)S(1)} %broadcast_in_dim.24), channel_id=1, replica_groups=mesh['zh'=6,'zl'=2,'x'=4,'c'=2,'y'=8] {'zl','x'}, dimensions={0} | all-to-all | bytes 2949120 | tf_op jit(solution)/shard_map/all_to_all | solution.py:14
  47.5 7.0 %collective-permute-start = (bf16[8,6,8,1920]{3,2,1,0:T(8,128)(2,1)S(1)}, bf16[8,6,8,1920]{3,2,1,0:T(8,128)(2,1)S(1)}, u32[]{:S(2)}, u32[]{:S(2)}) collective-permute-start(bf16[8,6,8,1920]{3,2,1,0:T(8,128)(2,1)S(1)} %all_to_all.11), channel_id=1, source_target_pairs={{0,8},{8,0},{1,9},{9,1},{2,10},{10,2},{3,11},{11,3},{4,12},{12,4},... | collective-permute-start | bytes 4423688 | tf_op jit(solution)/shard_map/ppermute | solution.py:58
  55.2 0.0 copy-done.2
  55.2 0.0 copy-done.1
  55.2 4.3 %compare_select_fusion = bf16[1920,1024]{1,0:T(8,128)(2,1)} fusion(bf16[1,1920,1024]{2,1,0:T(8,128)(2,1)} %param.6, bf16[1024]{0:T(1024)(128)(2,1)S(1)} %convert_element_type.66, bf16[1920]{0:T(1024)(128)(2,1)S(1)} %xor_convert_fusion), kind=kLoop, calls=%fused_computation | loop fusion | flops 3932160 | bytes 7870208 | tf_op jit(solution)/shard_map/jit(_where)/select_n | solution.py:59
  59.6 0.0 copy-start
  59.6 4.0 %convolution_convert_fusion.1 = bf16[1024,384]{0,1:T(8,128)(2,1)S(1)} fusion(bf16[384,1920]{1,0:T(8,128)(2,1)S(1)} %bitcast.44, bf16[1920,1024]{1,0:T(8,128)(2,1)} %compare_select_fusion), kind=kOutput, calls=%fused_computation.3 | convolution fusion | flops 1510342656 | bytes 6193152 | tf_op jit(solution)/shard_map/dot_general | solution.py:62
  63.6 0.0 collective-permute-done
  63.6 0.0 copy-done
  63.7 1.9 %broadcast_select_fusion.1 = (bf16[1024,384]{0,1:T(8,128)(2,1)S(1)}, bf16[1024,384]{0,1:T(8,128)(2,1)S(1)}) fusion(bf16[1024,384]{0,1:T(8,128)(2,1)S(1)} %convolution_convert_fusion.1, pred[]{:T(512)S(6)} %eq.26, bf16[384,1920]{1,0:T(8,128)(2,1)S(1)} %bitcast.48, bf16[1920,1024]{1,0:T(8,128)(2,1)S(1)} %copy-done), kind=kOutput, calls=%fused_computation.5 | convolution fusion | flops 1511129088 | bytes 7766017 | tf_op jit(solution)/shard_map/dot_general | solution.py:62
  65.5 0.1 pad_maximum_fusion
  65.7 0.2 copy.6
  65.8 0.1 constant_dynamic-slice_fusion.3
  66.0 5.1 %collective-permute-start.2 = (bf16[2,96,1024]{2,1,0:T(8,128)(2,1)S(1)}, bf16[2,96,1024]{2,1,0:T(8,128)(2,1)S(1)}, u32[]{:S(2)}, u32[]{:S(2)}) collective-permute-start(bf16[2,96,1024]{2,1,0:T(8,128)(2,1)S(1)} %pad_maximum_fusion.2), channel_id=1, source_target_pairs={{0,1},{1,2},{2,3},{3,4},{4,5},{5,6},{6,7},{7,0},{8,15},{9,8},{10,9... | collective-permute-start | bytes 1179656 | tf_op jit(solution)/shard_map/ppermute | solution.py:23
  71.1 3.8 %collective-permute-start.4 = (bf16[96,1024]{1,0:T(8,128)(2,1)S(1)}, bf16[96,1024]{1,0:T(8,128)(2,1)S(1)}, u32[]{:S(2)}, u32[]{:S(2)}) collective-permute-start(bf16[96,1024]{1,0:T(8,128)(2,1)S(1)} %get-tuple-element.6), channel_id=1, source_target_pairs={{0,2},{1,3},{2,4},{3,5},{4,6},{5,7},{6,0},{7,1},{8,14},{9,15},{10,... | collective-permute-start | bytes 589832 | tf_op jit(solution)/shard_map/ppermute | solution.py:23
  74.9 2.3 %collective-permute-start.1 = (bf16[2,96,1024]{2,1,0:T(8,128)(2,1)S(1)}, bf16[2,96,1024]{2,1,0:T(8,128)(2,1)S(1)}, u32[]{:S(2)}, u32[]{:S(2)}) collective-permute-start(bf16[2,96,1024]{2,1,0:T(8,128)(2,1)S(1)} %pad_maximum_fusion.1), channel_id=1, source_target_pairs={{0,7},{1,0},{2,1},{3,2},{4,3},{5,4},{6,5},{7,6},{8,9},{9,10},{10,1... | collective-permute-start | bytes 1179656 | tf_op jit(solution)/shard_map/ppermute | solution.py:23
  77.3 4.4 %collective-permute-done.4 = bf16[96,1024]{1,0:T(8,128)(2,1)S(1)} collective-permute-done((bf16[96,1024]{1,0:T(8,128)(2,1)S(1)}, bf16[96,1024]{1,0:T(8,128)(2,1)S(1)}, u32[]{:S(2)}, u32[]{:S(2)}) %collective-permute-start.4) | collective-permute-done | bytes 196640 | tf_op jit(solution)/shard_map/ppermute | solution.py:23
  81.7 0.0 collective-permute-done.2
  81.7 0.1 fusion
  81.8 5.9 %collective-permute-start.5 = (bf16[96,1024]{1,0:T(8,128)(2,1)S(1)}, bf16[96,1024]{1,0:T(8,128)(2,1)S(1)}, u32[]{:S(2)}, u32[]{:S(2)}) collective-permute-start(bf16[96,1024]{1,0:T(8,128)(2,1)S(1)} %fusion), channel_id=1, source_target_pairs={{0,2},{1,3},{2,4},{3,5},{4,6},{5,7},{6,0},{7,1},{8,14},{9,15},{10,... | collective-permute-start | bytes 589832 | tf_op jit(solution)/shard_map/ppermute | solution.py:23
  87.7 0.0 collective-permute-done.1
  87.7 0.1 fusion.3
  87.8 1.9 %collective-permute-start.3 = (bf16[96,1024]{1,0:T(8,128)(2,1)S(1)}, bf16[96,1024]{1,0:T(8,128)(2,1)S(1)}, u32[]{:S(2)}, u32[]{:S(2)}) collective-permute-start(bf16[96,1024]{1,0:T(8,128)(2,1)S(1)} %fusion.3), channel_id=1, source_target_pairs={{0,6},{1,7},{2,0},{3,1},{4,2},{5,3},{6,4},{7,5},{8,10},{9,11},{10,... | collective-permute-start | bytes 589832 | tf_op jit(solution)/shard_map/ppermute | solution.py:23
  89.7 1.4 %collective-permute-done.5 = bf16[96,1024]{1,0:T(8,128)(2,1)S(1)} collective-permute-done((bf16[96,1024]{1,0:T(8,128)(2,1)S(1)}, bf16[96,1024]{1,0:T(8,128)(2,1)S(1)}, u32[]{:S(2)}, u32[]{:S(2)}) %collective-permute-start.5) | collective-permute-done | bytes 196640 | tf_op jit(solution)/shard_map/ppermute | solution.py:23
  91.1 8.3 %collective-permute-done.3 = bf16[96,1024]{1,0:T(8,128)(2,1)S(1)} collective-permute-done((bf16[96,1024]{1,0:T(8,128)(2,1)S(1)}, bf16[96,1024]{1,0:T(8,128)(2,1)S(1)}, u32[]{:S(2)}, u32[]{:S(2)}) %collective-permute-start.3) | collective-permute-done | bytes 196640 | tf_op jit(solution)/shard_map/ppermute | solution.py:23
  99.4 0.8 fusion.2
  (4 shorter events, 0.1 us)
Async XLA Ops:
  25.4 29.7 %copy-start.2 = (s32[1024]{0:T(1024)S(1)}, s32[1024]{0:T(1024)}, u32[]{:S(2)}) copy-start(s32[1024]{0:T(1024)} %param.9) | copy-start | bytes 12292
  25.4 29.8 %copy-start.1 = (s32[1920]{0:T(1024)S(1)}, s32[1920]{0:T(1024)}, u32[]{:S(2)}) copy-start(s32[1920]{0:T(1024)} %param.8) | copy-start | bytes 23044
  47.5 16.1 %collective-permute-start = (bf16[8,6,8,1920]{3,2,1,0:T(8,128)(2,1)S(1)}, bf16[8,6,8,1920]{3,2,1,0:T(8,128)(2,1)S(1)}, u32[]{:S(2)}, u32[]{:S(2)}) collective-permute-start(bf16[8,6,8,1920]{3,2,1,0:T(8,128)(2,1)S(1)} %all_to_all.11), channel_id=1, source_target_pairs={{0,8},{8,0},{1,9},{9,1},{2,10},{10,2},{3,11},{11,3},{4,12},{12,4},... | collective-permute-start | bytes 4423688 | tf_op jit(solution)/shard_map/ppermute | solution.py:58
  59.6 4.1 %copy-start = (bf16[1920,1024]{1,0:T(8,128)(2,1)S(1)}, bf16[1920,1024]{1,0:T(8,128)(2,1)}, u32[]{:S(2)}) copy-start(bf16[1920,1024]{1,0:T(8,128)(2,1)} %compare_select_fusion) | copy-start | bytes 11796484
  66.0 15.7 %collective-permute-start.2 = (bf16[2,96,1024]{2,1,0:T(8,128)(2,1)S(1)}, bf16[2,96,1024]{2,1,0:T(8,128)(2,1)S(1)}, u32[]{:S(2)}, u32[]{:S(2)}) collective-permute-start(bf16[2,96,1024]{2,1,0:T(8,128)(2,1)S(1)} %pad_maximum_fusion.2), channel_id=1, source_target_pairs={{0,1},{1,2},{2,3},{3,4},{4,5},{5,6},{6,7},{7,0},{8,15},{9,8},{10,9... | collective-permute-start | bytes 1179656 | tf_op jit(solution)/shard_map/ppermute | solution.py:23
  71.1 10.6 %collective-permute-start.4 = (bf16[96,1024]{1,0:T(8,128)(2,1)S(1)}, bf16[96,1024]{1,0:T(8,128)(2,1)S(1)}, u32[]{:S(2)}, u32[]{:S(2)}) collective-permute-start(bf16[96,1024]{1,0:T(8,128)(2,1)S(1)} %get-tuple-element.6), channel_id=1, source_target_pairs={{0,2},{1,3},{2,4},{3,5},{4,6},{5,7},{6,0},{7,1},{8,14},{9,15},{10,... | collective-permute-start | bytes 589832 | tf_op jit(solution)/shard_map/ppermute | solution.py:23
  74.9 12.8 %collective-permute-start.1 = (bf16[2,96,1024]{2,1,0:T(8,128)(2,1)S(1)}, bf16[2,96,1024]{2,1,0:T(8,128)(2,1)S(1)}, u32[]{:S(2)}, u32[]{:S(2)}) collective-permute-start(bf16[2,96,1024]{2,1,0:T(8,128)(2,1)S(1)} %pad_maximum_fusion.1), channel_id=1, source_target_pairs={{0,7},{1,0},{2,1},{3,2},{4,3},{5,4},{6,5},{7,6},{8,9},{9,10},{10,1... | collective-permute-start | bytes 1179656 | tf_op jit(solution)/shard_map/ppermute | solution.py:23
  81.8 9.3 %collective-permute-start.5 = (bf16[96,1024]{1,0:T(8,128)(2,1)S(1)}, bf16[96,1024]{1,0:T(8,128)(2,1)S(1)}, u32[]{:S(2)}, u32[]{:S(2)}) collective-permute-start(bf16[96,1024]{1,0:T(8,128)(2,1)S(1)} %fusion), channel_id=1, source_target_pairs={{0,2},{1,3},{2,4},{3,5},{4,6},{5,7},{6,0},{7,1},{8,14},{9,15},{10,... | collective-permute-start | bytes 589832 | tf_op jit(solution)/shard_map/ppermute | solution.py:23
  87.8 11.6 %collective-permute-start.3 = (bf16[96,1024]{1,0:T(8,128)(2,1)S(1)}, bf16[96,1024]{1,0:T(8,128)(2,1)S(1)}, u32[]{:S(2)}, u32[]{:S(2)}) collective-permute-start(bf16[96,1024]{1,0:T(8,128)(2,1)S(1)} %fusion.3), channel_id=1, source_target_pairs={{0,6},{1,7},{2,0},{3,1},{4,2},{5,3},{6,4},{7,5},{8,10},{9,11},{10,... | collective-permute-start | bytes 589832 | tf_op jit(solution)/shard_map/ppermute | solution.py:23

commit v3 on v2

--- a/solution.py
+++ b/solution.py
@@ -37,14 +37,13 @@
     def part(offset):
         return lax.dynamic_index_in_dim(terms, (y + sign * offset + NY) % NY, 0, keepdims=False)
 
-    near_down = mirrored(jnp.stack([part(-1), part(-3)]), -1)
-    near_up = mirrored(jnp.stack([part(1), part(3)]), 1)
-    far = mirrored(part(4), 2)
-    down = plus(part(-2), near_down[1])
-    got_down = mirrored(down, -2)
-    up = plus(part(2), near_up[1], far)
-    got_up = mirrored(up, 2)
-    return plus(part(0), near_down[0], near_up[0], got_down, got_up)
+    part = dict(zip(range(-3, 5), tie(tuple(part(offset) for offset in range(-3, 5)))))
+    far = mirrored(part[4], 1)
+    near_down = mirrored(jnp.stack([part[-1], part[-3]]), -1)
+    near_up = mirrored(jnp.stack([part[1], plus(part[3], far)]), 1)
+    got_down = mirrored(plus(part[-2], near_down[1]), -2)
+    got_up = mirrored(plus(part[2], near_up[1]), 2)
+    return plus(part[0], near_down[0], near_up[0], got_down, got_up)
 
 
 def on_device(amps, cycle_w, occ_irrep, vir_irrep, col_irrep):
@@ -53,10 +52,10 @@
     allowed = pair_sym.astype(BF16)[:, None] == col_irrep.astype(BF16)[None, :]
     weights = cycle_w.reshape(-1, cycle_w.shape[2])
     block = amps.reshape(amps.shape[0], -1)
-    along_z = gather(block, "zh", ZH)
+    masked = jnp.where(allowed, weights, jnp.zeros((), weights.dtype))
+    along_z, masked = tie((gather(block, "zh", ZH), masked))
     mine = gather(along_z, ("zl", "x"), ZL * NX)
     theirs = lax.ppermute(mine, "c", [(0, 1), (1, 0)])
-    masked = tie(jnp.where(allowed, weights, jnp.zeros((), weights.dtype)))
 
     def product(rows):
         part = jnp.dot(rows.reshape(-1, rows.shape[-1]), masked, preferred_element_type=F32).astype(BF16)

time: 101 us -> 95.6 us (0.947)
  the two profiles are of different devices: /device:TPU:1 before, /device:TPU:32 now
where the time goes in v3:
time: 95.6 us; the launch traced here: 95.1 us
  starting transfers between devices  30.9 us (32%)
  waiting for transfers between devices  25.9 us (27%)
  blocking collectives  22.6 us (24%)
  other arithmetic  6.94 us (7%)
  matrix products  5.9 us (6%)
  local copies, waits for them, and re-layouts  1.9 us (2%)
    all_to_all x1, blocking collectives, gather(): return lax.all_to_all(copies, axis, 0, 0, tiled=False)  22.6 us
    ppermute x5, waiting for transfers between devices, mirrored(): return lax.ppermute(array, ('c', 'y'), pairs)  19.1 us
    all_to_all x1, starting transfers between devices, gather(): return lax.all_to_all(copies, axis, 0, 0, tiled=False)  14.5 us
    ppermute x5, starting transfers between devices, mirrored(): return lax.ppermute(array, ('c', 'y'), pairs)  14.5 us
    all_to_all x1, waiting for transfers between devices, gather(): return lax.all_to_all(copies, axis, 0, 0, tiled=False)  6.84 us
    dot_general x2, matrix products, product(): jnp.dot(rows.reshape(-1, rows.shape[-1]), masked, preferred_element_type=...  5.9 us
    select_n x1, other arithmetic, on_device(): masked = jnp.where(allowed, weights, jnp.zeros((), weights.dtype))  4.34 us
  transfers between devices with their start and end apart: 7, of which 5 were waited for; matrix products, arithmetic and copies ran while one was open for 11% of the time, Pallas kernels for 0%

profile of v3, /device:TPU:32, one launch (start us, length us, event | category | flops | bytes accessed | tf_op | source)
XLA Modules:
  0.0 95.1 jit_solution(12969927274288382638)
XLA Ops:
  0.0 1.4 %broadcast_in_dim.11 = bf16[6,8,1920]{2,1,0:T(8,128)(2,1)} broadcast(bf16[8,1920]{1,0:T(8,128)(2,1)} %bitcast.70), dimensions={1,2} | broadcast | bytes 215040 | tf_op jit(solution)/shard_map/broadcast_in_dim | solution.py:13
  1.4 14.5 %all-to-all-start = ((bf16[6,8,1920]{2,1,0:T(8,128)(2,1)}), bf16[6,8,1920]{2,1,0:T(8,128)(2,1)S(1)}, u32[]{:S(2)}, u32[]{:S(2)}) async-start(bf16[6,8,1920]{2,1,0:T(8,128)(2,1)} %broadcast_in_dim.11), calls=%async_computation | async-start | bytes 368640 | tf_op jit(solution)/shard_map/all_to_all | solution.py:14
  15.9 0.7 convert_element_type.72
  17.3 0.7 xor_convert_fusion
  18.0 4.3 %compare_select_fusion = bf16[1920,1024]{1,0:T(8,128)(2,1)} fusion(bf16[1,1920,1024]{2,1,0:T(8,128)(2,1)} %param.6, bf16[1024]{0:T(1024)(128)(2,1)S(1)} %convert_element_type.72, bf16[1920]{0:T(1024)(128)(2,1)S(1)} %xor_convert_fusion), kind=kLoop, calls=%fused_computation | loop fusion | flops 3932160 | bytes 7870208 | tf_op jit(solution)/shard_map/jit(_where)/select_n | solution.py:55
  22.3 6.8 %all-to-all-done = bf16[6,8,1920]{2,1,0:T(8,128)(2,1)S(1)} async-done(((bf16[6,8,1920]{2,1,0:T(8,128)(2,1)}), bf16[6,8,1920]{2,1,0:T(8,128)(2,1)S(1)}, u32[]{:S(2)}, u32[]{:S(2)}) %all-to-all-start) | async-done | bytes 184352 | tf_op jit(solution)/shard_map/all_to_all | solution.py:14
  29.2 0.1 broadcast_in_dim.24
  29.3 22.6 %all_to_all.10 = bf16[8,6,8,1920]{3,2,1,0:T(8,128)(2,1)S(1)} all-to-all(bf16[8,6,8,1920]{3,2,1,0:T(8,128)(2,1)S(1)} %broadcast_in_dim.24), channel_id=1, replica_groups=mesh['zh'=6,'zl'=2,'x'=4,'c'=2,'y'=8] {'zl','x'}, dimensions={0} | all-to-all | bytes 2949120 | tf_op jit(solution)/shard_map/all_to_all | solution.py:14
  51.9 1.9 %collective-permute-start = (bf16[8,6,8,1920]{3,2,1,0:T(8,128)(2,1)S(1)}, bf16[8,6,8,1920]{3,2,1,0:T(8,128)(2,1)S(1)}, u32[]{:S(2)}, u32[]{:S(2)}) collective-permute-start(bf16[8,6,8,1920]{3,2,1,0:T(8,128)(2,1)S(1)} %all_to_all.10), channel_id=1, source_target_pairs={{0,8},{8,0},{1,9},{9,1},{2,10},{10,2},{3,11},{11,3},{4,12},{12,4},... | collective-permute-start | bytes 4423688 | tf_op jit(solution)/shard_map/ppermute | solution.py:58
  53.9 0.0 copy-start
  53.9 4.0 %convolution_convert_fusion.1 = bf16[384,1024]{1,0:T(8,128)(2,1)S(1)} fusion(bf16[384,1920]{1,0:T(8,128)(2,1)S(1)} %bitcast.64, bf16[1920,1024]{1,0:T(8,128)(2,1)} %compare_select_fusion), kind=kOutput, calls=%fused_computation.3 | convolution fusion | flops 1510342656 | bytes 6193152 | tf_op jit(solution)/shard_map/dot_general | solution.py:61
  58.0 0.0 collective-permute-done
  58.0 0.0 copy-done
  58.0 1.9 %broadcast_select_fusion.1 = (bf16[384,1024]{1,0:T(8,128)(2,1)S(1)}, bf16[384,1024]{1,0:T(8,128)(2,1)S(1)}) fusion(bf16[384,1024]{1,0:T(8,128)(2,1)S(1)} %convolution_convert_fusion.1, pred[]{:T(512)S(6)} %eq.26, bf16[384,1920]{1,0:T(8,128)(2,1)S(1)} %bitcast.71, bf16[1920,1024]{1,0:T(8,128)(2,1)S(1)} %copy-done), kind=kOutput, calls=%fused_computation.7 | convolution fusion | flops 1511129088 | bytes 7766017 | tf_op jit(solution)/shard_map/dot_general | solution.py:61
  59.9 0.2 copy_bitcast_fusion
  60.0 0.1 pad_maximum_fusion
  60.2 0.2 dynamic-slice_bitcast_fusion
  60.4 2.6 %collective-permute-start.2 = (bf16[96,1024]{1,0:T(8,128)(2,1)S(1)}, bf16[96,1024]{1,0:T(8,128)(2,1)S(1)}, u32[]{:S(2)}, u32[]{:S(2)}) collective-permute-start(bf16[96,1024]{1,0:T(8,128)(2,1)S(1)} %get-tuple-element.22), channel_id=1, source_target_pairs={{0,1},{1,2},{2,3},{3,4},{4,5},{5,6},{6,7},{7,0},{8,15},{9,8},{10,9... | collective-permute-start | bytes 589832 | tf_op jit(solution)/shard_map/ppermute | solution.py:23
  63.0 4.5 %collective-permute-start.1 = (bf16[2,96,1024]{2,1,0:T(8,128)(2,1)S(1)}, bf16[2,96,1024]{2,1,0:T(8,128)(2,1)S(1)}, u32[]{:S(2)}, u32[]{:S(2)}) collective-permute-start(bf16[2,96,1024]{2,1,0:T(8,128)(2,1)S(1)} %pad_maximum_fusion.1), channel_id=1, source_target_pairs={{0,7},{1,0},{2,1},{3,2},{4,3},{5,4},{6,5},{7,6},{8,9},{9,10},{10,1... | collective-permute-start | bytes 1179656 | tf_op jit(solution)/shard_map/ppermute | solution.py:23
  67.5 2.0 %collective-permute-done.2 = bf16[96,1024]{1,0:T(8,128)(2,1)S(1)} collective-permute-done((bf16[96,1024]{1,0:T(8,128)(2,1)S(1)}, bf16[96,1024]{1,0:T(8,128)(2,1)S(1)}, u32[]{:S(2)}, u32[]{:S(2)}) %collective-permute-start.2) | collective-permute-done | bytes 196640 | tf_op jit(solution)/shard_map/ppermute | solution.py:23
  69.7 1.9 %collective-permute-start.3 = (bf16[2,96,1024]{2,1,0:T(8,128)(2,1)S(1)}, bf16[2,96,1024]{2,1,0:T(8,128)(2,1)S(1)}, u32[]{:S(2)}, u32[]{:S(2)}) collective-permute-start(bf16[2,96,1024]{2,1,0:T(8,128)(2,1)S(1)} %pad_maximum_fusion.2), channel_id=1, source_target_pairs={{0,1},{1,2},{2,3},{3,4},{4,5},{5,6},{6,7},{7,0},{8,15},{9,8},{10,9... | collective-permute-start | bytes 1179656 | tf_op jit(solution)/shard_map/ppermute | solution.py:23
  71.6 2.8 %collective-permute-done.1 = bf16[2,96,1024]{2,1,0:T(8,128)(2,1)S(1)} collective-permute-done((bf16[2,96,1024]{2,1,0:T(8,128)(2,1)S(1)}, bf16[2,96,1024]{2,1,0:T(8,128)(2,1)S(1)}, u32[]{:S(2)}, u32[]{:S(2)}) %collective-permute-start.1) | collective-permute-done | bytes 393248 | tf_op jit(solution)/shard_map/ppermute | solution.py:23
  74.5 3.6 %collective-permute-start.4 = (bf16[96,1024]{1,0:T(8,128)(2,1)S(1)}, bf16[96,1024]{1,0:T(8,128)(2,1)S(1)}, u32[]{:S(2)}, u32[]{:S(2)}) collective-permute-start(bf16[96,1024]{1,0:T(8,128)(2,1)S(1)} %fusion.1), channel_id=1, source_target_pairs={{0,6},{1,7},{2,0},{3,1},{4,2},{5,3},{6,4},{7,5},{8,10},{9,11},{10,... | collective-permute-start | bytes 589832 | tf_op jit(solution)/shard_map/ppermute | solution.py:23
  78.0 6.4 %collective-permute-done.3 = bf16[2,96,1024]{2,1,0:T(8,128)(2,1)S(1)} collective-permute-done((bf16[2,96,1024]{2,1,0:T(8,128)(2,1)S(1)}, bf16[2,96,1024]{2,1,0:T(8,128)(2,1)S(1)}, u32[]{:S(2)}, u32[]{:S(2)}) %collective-permute-start.3) | collective-permute-done | bytes 393248 | tf_op jit(solution)/shard_map/ppermute | solution.py:23
  84.5 1.9 %collective-permute-start.5 = (bf16[96,1024]{1,0:T(8,128)(2,1)S(1)}, bf16[96,1024]{1,0:T(8,128)(2,1)S(1)}, u32[]{:S(2)}, u32[]{:S(2)}) collective-permute-start(bf16[96,1024]{1,0:T(8,128)(2,1)S(1)} %fusion), channel_id=1, source_target_pairs={{0,2},{1,3},{2,4},{3,5},{4,6},{5,7},{6,0},{7,1},{8,14},{9,15},{10,... | collective-permute-start | bytes 589832 | tf_op jit(solution)/shard_map/ppermute | solution.py:23
  86.5 0.0 collective-permute-done.4
  86.5 7.7 %collective-permute-done.5 = bf16[96,1024]{1,0:T(8,128)(2,1)S(1)} collective-permute-done((bf16[96,1024]{1,0:T(8,128)(2,1)S(1)}, bf16[96,1024]{1,0:T(8,128)(2,1)S(1)}, u32[]{:S(2)}, u32[]{:S(2)}) %collective-permute-start.5) | collective-permute-done | bytes 196640 | tf_op jit(solution)/shard_map/ppermute | solution.py:23
  94.2 0.8 fusion.4
  (5 shorter events, 0.2 us)
Async XLA Ops:
  1.4 27.7 %all-to-all-start = ((bf16[6,8,1920]{2,1,0:T(8,128)(2,1)}), bf16[6,8,1920]{2,1,0:T(8,128)(2,1)S(1)}, u32[]{:S(2)}, u32[]{:S(2)}) async-start(bf16[6,8,1920]{2,1,0:T(8,128)(2,1)} %broadcast_in_dim.11), calls=%async_computation | async-start | bytes 368640 | tf_op jit(solution)/shard_map/all_to_all | solution.py:14
  51.9 6.1 %collective-permute-start = (bf16[8,6,8,1920]{3,2,1,0:T(8,128)(2,1)S(1)}, bf16[8,6,8,1920]{3,2,1,0:T(8,128)(2,1)S(1)}, u32[]{:S(2)}, u32[]{:S(2)}) collective-permute-start(bf16[8,6,8,1920]{3,2,1,0:T(8,128)(2,1)S(1)} %all_to_all.10), channel_id=1, source_target_pairs={{0,8},{8,0},{1,9},{9,1},{2,10},{10,2},{3,11},{11,3},{4,12},{12,4},... | collective-permute-start | bytes 4423688 | tf_op jit(solution)/shard_map/ppermute | solution.py:58
  53.9 4.1 %copy-start = (bf16[1920,1024]{1,0:T(8,128)(2,1)S(1)}, bf16[1920,1024]{1,0:T(8,128)(2,1)}, u32[]{:S(2)}) copy-start(bf16[1920,1024]{1,0:T(8,128)(2,1)} %compare_select_fusion) | copy-start | bytes 11796484
  60.4 9.1 %collective-permute-start.2 = (bf16[96,1024]{1,0:T(8,128)(2,1)S(1)}, bf16[96,1024]{1,0:T(8,128)(2,1)S(1)}, u32[]{:S(2)}, u32[]{:S(2)}) collective-permute-start(bf16[96,1024]{1,0:T(8,128)(2,1)S(1)} %get-tuple-element.22), channel_id=1, source_target_pairs={{0,1},{1,2},{2,3},{3,4},{4,5},{5,6},{6,7},{7,0},{8,15},{9,8},{10,9... | collective-permute-start | bytes 589832 | tf_op jit(solution)/shard_map/ppermute | solution.py:23
  63.0 11.4 %collective-permute-start.1 = (bf16[2,96,1024]{2,1,0:T(8,128)(2,1)S(1)}, bf16[2,96,1024]{2,1,0:T(8,128)(2,1)S(1)}, u32[]{:S(2)}, u32[]{:S(2)}) collective-permute-start(bf16[2,96,1024]{2,1,0:T(8,128)(2,1)S(1)} %pad_maximum_fusion.1), channel_id=1, source_target_pairs={{0,7},{1,0},{2,1},{3,2},{4,3},{5,4},{6,5},{7,6},{8,9},{9,10},{10,1... | collective-permute-start | bytes 1179656 | tf_op jit(solution)/shard_map/ppermute | solution.py:23
  69.7 14.8 %collective-permute-start.3 = (bf16[2,96,1024]{2,1,0:T(8,128)(2,1)S(1)}, bf16[2,96,1024]{2,1,0:T(8,128)(2,1)S(1)}, u32[]{:S(2)}, u32[]{:S(2)}) collective-permute-start(bf16[2,96,1024]{2,1,0:T(8,128)(2,1)S(1)} %pad_maximum_fusion.2), channel_id=1, source_target_pairs={{0,1},{1,2},{2,3},{3,4},{4,5},{5,6},{6,7},{7,0},{8,15},{9,8},{10,9... | collective-permute-start | bytes 1179656 | tf_op jit(solution)/shard_map/ppermute | solution.py:23
  74.5 12.0 %collective-permute-start.4 = (bf16[96,1024]{1,0:T(8,128)(2,1)S(1)}, bf16[96,1024]{1,0:T(8,128)(2,1)S(1)}, u32[]{:S(2)}, u32[]{:S(2)}) collective-permute-start(bf16[96,1024]{1,0:T(8,128)(2,1)S(1)} %fusion.1), channel_id=1, source_target_pairs={{0,6},{1,7},{2,0},{3,1},{4,2},{5,3},{6,4},{7,5},{8,10},{9,11},{10,... | collective-permute-start | bytes 589832 | tf_op jit(solution)/shard_map/ppermute | solution.py:23
  84.5 9.7 %collective-permute-start.5 = (bf16[96,1024]{1,0:T(8,128)(2,1)S(1)}, bf16[96,1024]{1,0:T(8,128)(2,1)S(1)}, u32[]{:S(2)}, u32[]{:S(2)}) collective-permute-start(bf16[96,1024]{1,0:T(8,128)(2,1)S(1)} %fusion), channel_id=1, source_target_pairs={{0,2},{1,3},{2,4},{3,5},{4,6},{5,7},{6,0},{7,1},{8,14},{9,15},{10,... | collective-permute-start | bytes 589832 | tf_op jit(solution)/shard_map/ppermute | solution.py:23

commit v4 on v3

--- a/solution.py
+++ b/solution.py
@@ -1,6 +1,8 @@
 import jax
 import jax.numpy as jnp
 from jax import lax
+from jax.experimental import pallas as pl
+from jax.experimental.pallas import tpu as pltpu
 from jax.sharding import Mesh, PartitionSpec as P
 
 ZH, ZL, NX, NC, NY = 6, 2, 4, 2, 8
@@ -12,6 +14,15 @@
 def gather(block, axis, size):
     copies = jnp.broadcast_to(block[None], (size,) + block.shape)
     return lax.all_to_all(copies, axis, 0, 0, tiled=False)
+
+
+ORDER = [5, 4, 0, 1, 2, 3]
+
+
+def gather_z(block):
+    copies = jnp.broadcast_to(block[None], (ZH,) + block.shape)
+    got = lax.all_to_all(copies, "zh", 0, 0, tiled=False, axis_index_groups=[ORDER])
+    return jnp.stack([got[ORDER.index(i)] for i in range(ZH)])
 
 
 def mirrored(array, step):
@@ -46,15 +57,43 @@
     return plus(part[0], near_down[0], near_up[0], got_down, got_up)
 
 
+def mask_rows(occ_ref, vir_ref, col_ref, weights_ref, out_ref):
+    lanes = vir_ref.shape[-1]
+    for i in range(weights_ref.shape[0] // lanes):
+        sym = jnp.bitwise_xor(vir_ref[0, i:i + 1, :], occ_ref[0]).astype(F32)
+        sym = jnp.broadcast_to(sym, (lanes, lanes)).T.astype(BF16)
+        rows = pl.ds(i * lanes, lanes)
+        for j in range(weights_ref.shape[1] // lanes):
+            cols = pl.ds(j * lanes, lanes)
+            allowed = sym == col_ref[j:j + 1, :].astype(F32).astype(BF16)
+            out_ref[rows, cols] = jnp.where(allowed, weights_ref[rows, cols], jnp.zeros((), BF16))
+
+
+def mask_weights(occ_irrep, vir_irrep, col_irrep, weights):
+    steps, lanes = 5, 128
+    depth, width = weights.shape
+    return pl.pallas_call(
+        mask_rows,
+        out_shape=jax.ShapeDtypeStruct(weights.shape, weights.dtype),
+        grid=(steps,),
+        in_specs=[
+            pl.BlockSpec(memory_space=pltpu.SMEM),
+            pl.BlockSpec((1, depth // steps // lanes, lanes), lambda i: (i, 0, 0)),
+            pl.BlockSpec((width // lanes, lanes), lambda i: (0, 0)),
+            pl.BlockSpec((depth // steps, width), lambda i: (i, 0)),
+        ],
+        out_specs=pl.BlockSpec((depth // steps, width), lambda i: (i, 0)),
+        compiler_params=pltpu.CompilerParams(vmem_limit_bytes=8 << 20),
+        cost_estimate=pl.CostEstimate(flops=depth * width, bytes_accessed=4 * depth * width, transcendentals=0),
+    )(occ_irrep, vir_irrep.reshape(steps, -1, lanes), col_irrep.reshape(-1, lanes), weights)
+
+
 def on_device(amps, cycle_w, occ_irrep, vir_irrep, col_irrep):
     c = lax.axis_index("c")
-    pair_sym = jnp.bitwise_xor(occ_irrep[:, None], vir_irrep[None, :]).reshape(-1)
-    allowed = pair_sym.astype(BF16)[:, None] == col_irrep.astype(BF16)[None, :]
     weights = cycle_w.reshape(-1, cycle_w.shape[2])
     block = amps.reshape(amps.shape[0], -1)
-    masked = jnp.where(allowed, weights, jnp.zeros((), weights.dtype))
-    along_z, masked = tie((gather(block, "zh", ZH), masked))
-    mine = gather(along_z, ("zl", "x"), ZL * NX)
+    masked = mask_weights(occ_irrep, vir_irrep, col_irrep, weights)
+    mine, masked = tie((gather(gather_z(block), ("zl", "x"), ZL * NX), masked))
     theirs = lax.ppermute(mine, "c", [(0, 1), (1, 0)])
 
     def product(rows):

time: 95.6 us -> 92.2 us (0.964)
  starting transfers between devices: 30.9 us -> 20.8 us
  other arithmetic: 6.94 us -> 1.24 us
  local copies, waits for them, and re-layouts: 1.9 us -> 6.35 us
  waiting for transfers between devices: 25.9 us -> 29.4 us
  blocking collectives: 22.6 us -> 25.8 us
  Pallas kernels: 0 us -> 1.19 us
    all_to_all x1, starting transfers between devices: 14.5 us -> 4.43 us  [gather(): return lax.all_to_all(copies, axis, 0, 0, tiled=False)]
    select_n x1 -> x0, other arithmetic: 4.34 us -> none  [on_device(): masked = jnp.where(allowed, weights, jnp.zeros((), weights.dtype))]
    unnamed x2 -> x10, local copies, waits for them, and re-layouts: 0.01 us -> 3.97 us
    all_to_all x1, waiting for transfers between devices: 6.84 us -> 10.3 us  [gather(): return lax.all_to_all(copies, axis, 0, 0, tiled=False)]
    all_to_all x1, blocking collectives: 22.6 us -> 25.8 us  [gather_z(): lax.all_to_all(copies, 'zh', 0, 0, tiled=False, axis_index_groups=[ORDER])]
    convert_element_type x2 -> x0, other arithmetic: 1.39 us -> none  [on_device(): allowed = pair_sym.astype(BF16)[:, None] == col_irrep.astype(BF16)[None, :]]
    pallas_call x0 -> x1, Pallas kernels: none -> 1.19 us  [mask_weights(): pl.pallas_call(mask_rows, out_shape=jax.ShapeDtypeStruct(weights.shape, w...]
  transfers between devices with their start and end apart: 7 -> 7, of which waited for: 5 -> 5; matrix products, arithmetic and copies ran while one was open for 11% -> 5% of each run, Pallas kernels for 0% -> 1%
where the time goes in v4:
time: 92.2 us; the launch traced here: 91.7 us
  waiting for transfers between devices  29.4 us (32%)
  blocking collectives  25.8 us (28%)
  starting transfers between devices  20.8 us (23%)
  local copies, waits for them, and re-layouts  6.35 us (7%)
  matrix products  5.91 us (6%)
  other arithmetic  1.24 us (1%)
  Pallas kernels  1.19 us (1%)
  between operations  0.99 us (1%)
    all_to_all x1, blocking collectives, gather_z(): lax.all_to_all(copies, 'zh', 0, 0, tiled=False, axis_index_groups=[ORDER])  25.8 us
    ppermute x5, waiting for transfers between devices, mirrored(): return lax.ppermute(array, ('c', 'y'), pairs)  19.1 us
    ppermute x5, starting transfers between devices, mirrored(): return lax.ppermute(array, ('c', 'y'), pairs)  14.4 us
    all_to_all x1, waiting for transfers between devices, gather(): return lax.all_to_all(copies, axis, 0, 0, tiled=False)  10.3 us
    dot_general x2, matrix products, product(): jnp.dot(rows.reshape(-1, rows.shape[-1]), masked, preferred_element_type=...  5.91 us
    all_to_all x1, starting transfers between devices, gather(): return lax.all_to_all(copies, axis, 0, 0, tiled=False)  4.43 us
    unnamed x10, local copies, waits for them, and re-layouts  3.97 us
    ppermute x1, starting transfers between devices, on_device(): theirs = lax.ppermute(mine, 'c', [(0, 1), (1, 0)])  1.91 us
  transfers between devices with their start and end apart: 7, of which 5 were waited for; matrix products, arithmetic and copies ran while one was open for 5% of the time, Pallas kernels for 1%

profile of v4, /device:TPU:32, one launch (start us, length us, event | category | flops | bytes accessed | tf_op | source)
XLA Modules:
  0.0 91.7 jit_solution(10922039075052367928)
XLA Ops:
  0.0 0.8 broadcast_in_dim.14
  0.8 25.8 %all_to_all.10 = bf16[6,8,1920]{2,1,0:T(8,128)(2,1)S(1)} all-to-all(bf16[6,8,1920]{2,1,0:T(8,128)(2,1)S(1)} %broadcast_in_dim.14), channel_id=1, replica_groups={{640,512,0,128,256,384},{641,513,1,129,257,385},{642,514,2,130,258,386}..., dimensions={0} | all-to-all | bytes 368640 | tf_op jit(solution)/shard_map/all_to_all | solution.py:24
  26.7 1.2 %broadcast_in_dim.15 = bf16[8,6,8,1920]{3,2,1,0:T(8,128)(2,1)} broadcast(bf16[6,8,1920]{2,1,0:T(8,128)(2,1)S(1)} %pad_maximum_fusion.3), dimensions={1,2,3} | broadcast | bytes 1658880 | tf_op jit(solution)/shard_map/broadcast_in_dim | solution.py:15
  27.9 0.0 copy-start.4
  27.9 0.0 copy-start.3
  27.9 4.4 %all-to-all-start.1 = ((bf16[8,6,8,1920]{3,2,1,0:T(8,128)(2,1)}), bf16[8,6,8,1920]{3,2,1,0:T(8,128)(2,1)S(1)}, u32[]{:S(2)}, u32[]{:S(2)}) async-start(bf16[8,6,8,1920]{3,2,1,0:T(8,128)(2,1)} %broadcast_in_dim.15), calls=%async_computation.1 | async-start | bytes 2949120 | tf_op jit(solution)/shard_map/all_to_all | solution.py:16
  33.0 0.0 copy-done.4
  33.0 0.0 copy-done.3
  33.0 0.0 copy-start
  33.0 2.1 %copy-done = bf16[1,1920,1024]{2,1,0:T(8,128)(2,1)S(1)} copy-done((bf16[1,1920,1024]{2,1,0:T(8,128)(2,1)S(1)}, bf16[1,1920,1024]{2,1,0:T(8,128)(2,1)}, u32[]{:S(2)}) %copy-start) | copy-done | bytes 3932184
  35.1 1.2 %shard_map.55 = bf16[1920,1024]{1,0:T(8,128)(2,1)S(1)} custom-call(s32[1]{0:T(128)S(6)} %copy.10.occ_ref, s32[5,3,128]{2,1,0:T(4,128)S(1)} %reshape.34.vir_ref, s32[8,128]{1,0:T(8,128)S(1)} %bitcast.62, bf16[1920,1024]{1,0:T(8,128)(2,1)S(1)} %bitcast.61), custom_call_target="tpu_custom_call" | custom-call | flops 1966080 | bytes 7864320 | tf_op jit(solution)/shard_map/pallas_call | solution.py:75
  36.3 0.0 copy-start.1
  36.3 1.9 %copy-done.1 = bf16[1920,1024]{1,0:T(8,128)(2,1)} copy-done((bf16[1920,1024]{1,0:T(8,128)(2,1)}, bf16[1920,1024]{1,0:T(8,128)(2,1)S(1)}, u32[]{:S(2)}) %copy-start.1) | copy-done | bytes 3932184
  38.2 10.3 %all-to-all-done.1 = bf16[8,6,8,1920]{3,2,1,0:T(8,128)(2,1)S(1)} async-done(((bf16[8,6,8,1920]{3,2,1,0:T(8,128)(2,1)}), bf16[8,6,8,1920]{3,2,1,0:T(8,128)(2,1)S(1)}, u32[]{:S(2)}, u32[]{:S(2)}) %all-to-all-start.1) | async-done | bytes 1474592 | tf_op jit(solution)/shard_map/all_to_all | solution.py:16
  48.5 1.9 %collective-permute-start = (bf16[8,6,8,1920]{3,2,1,0:T(8,128)(2,1)S(1)}, bf16[8,6,8,1920]{3,2,1,0:T(8,128)(2,1)S(1)}, u32[]{:S(2)}, u32[]{:S(2)}) collective-permute-start(bf16[8,6,8,1920]{3,2,1,0:T(8,128)(2,1)S(1)} %all-to-all-done.1), channel_id=1, source_target_pairs={{0,8},{8,0},{1,9},{9,1},{2,10},{10,2},{3,11},{11,3},{4,12},{12,4},... | collective-permute-start | bytes 4423688 | tf_op jit(solution)/shard_map/ppermute | solution.py:97
  50.5 0.0 copy-start.2
  50.6 4.0 %convolution_convert_fusion.1 = bf16[384,1024]{1,0:T(8,128)(2,1)S(1)} fusion(bf16[384,1920]{1,0:T(8,128)(2,1)S(1)} %bitcast.64, bf16[1920,1024]{1,0:T(8,128)(2,1)} %copy-done.1), kind=kOutput, calls=%fused_computation.2 | convolution fusion | flops 1510342656 | bytes 6193152 | tf_op jit(solution)/shard_map/dot_general | solution.py:100
  54.6 0.0 collective-permute-done
  54.6 0.0 copy-done.2
  54.6 1.9 %broadcast_select_fusion.1 = (bf16[384,1024]{1,0:T(8,128)(2,1)S(1)}, bf16[384,1024]{1,0:T(8,128)(2,1)S(1)}) fusion(bf16[384,1024]{1,0:T(8,128)(2,1)S(1)} %convolution_convert_fusion.1, pred[]{:T(512)S(6)} %eq.13, bf16[384,1920]{1,0:T(8,128)(2,1)S(1)} %bitcast.71, bf16[1920,1024]{1,0:T(8,128)(2,1)S(1)} %copy-done.2), kind=kOutput, calls=%fused_computation.6 | convolution fusion | flops 1511129088 | bytes 7766017 | tf_op jit(solution)/shard_map/dot_general | solution.py:100
  56.5 0.2 copy_bitcast_fusion
  56.7 0.1 pad_maximum_fusion
  56.8 0.2 dynamic-slice_bitcast_fusion
  57.0 2.6 %collective-permute-start.2 = (bf16[96,1024]{1,0:T(8,128)(2,1)S(1)}, bf16[96,1024]{1,0:T(8,128)(2,1)S(1)}, u32[]{:S(2)}, u32[]{:S(2)}) collective-permute-start(bf16[96,1024]{1,0:T(8,128)(2,1)S(1)} %get-tuple-element.22), channel_id=1, source_target_pairs={{0,1},{1,2},{2,3},{3,4},{4,5},{5,6},{6,7},{7,0},{8,15},{9,8},{10,9... | collective-permute-start | bytes 589832 | tf_op jit(solution)/shard_map/ppermute | solution.py:34
  59.7 4.5 %collective-permute-start.1 = (bf16[2,96,1024]{2,1,0:T(8,128)(2,1)S(1)}, bf16[2,96,1024]{2,1,0:T(8,128)(2,1)S(1)}, u32[]{:S(2)}, u32[]{:S(2)}) collective-permute-start(bf16[2,96,1024]{2,1,0:T(8,128)(2,1)S(1)} %pad_maximum_fusion.1), channel_id=1, source_target_pairs={{0,7},{1,0},{2,1},{3,2},{4,3},{5,4},{6,5},{7,6},{8,9},{9,10},{10,1... | collective-permute-start | bytes 1179656 | tf_op jit(solution)/shard_map/ppermute | solution.py:34
  64.1 2.0 %collective-permute-done.2 = bf16[96,1024]{1,0:T(8,128)(2,1)S(1)} collective-permute-done((bf16[96,1024]{1,0:T(8,128)(2,1)S(1)}, bf16[96,1024]{1,0:T(8,128)(2,1)S(1)}, u32[]{:S(2)}, u32[]{:S(2)}) %collective-permute-start.2) | collective-permute-done | bytes 196640 | tf_op jit(solution)/shard_map/ppermute | solution.py:34
  66.3 1.9 %collective-permute-start.3 = (bf16[2,96,1024]{2,1,0:T(8,128)(2,1)S(1)}, bf16[2,96,1024]{2,1,0:T(8,128)(2,1)S(1)}, u32[]{:S(2)}, u32[]{:S(2)}) collective-permute-start(bf16[2,96,1024]{2,1,0:T(8,128)(2,1)S(1)} %pad_maximum_fusion.2), channel_id=1, source_target_pairs={{0,1},{1,2},{2,3},{3,4},{4,5},{5,6},{6,7},{7,0},{8,15},{9,8},{10,9... | collective-permute-start | bytes 1179656 | tf_op jit(solution)/shard_map/ppermute | solution.py:34
  68.2 2.9 %collective-permute-done.1 = bf16[2,96,1024]{2,1,0:T(8,128)(2,1)S(1)} collective-permute-done((bf16[2,96,1024]{2,1,0:T(8,128)(2,1)S(1)}, bf16[2,96,1024]{2,1,0:T(8,128)(2,1)S(1)}, u32[]{:S(2)}, u32[]{:S(2)}) %collective-permute-start.1) | collective-permute-done | bytes 393248 | tf_op jit(solution)/shard_map/ppermute | solution.py:34
  71.1 3.6 %collective-permute-start.4 = (bf16[96,1024]{1,0:T(8,128)(2,1)S(1)}, bf16[96,1024]{1,0:T(8,128)(2,1)S(1)}, u32[]{:S(2)}, u32[]{:S(2)}) collective-permute-start(bf16[96,1024]{1,0:T(8,128)(2,1)S(1)} %fusion.1), channel_id=1, source_target_pairs={{0,6},{1,7},{2,0},{3,1},{4,2},{5,3},{6,4},{7,5},{8,10},{9,11},{10,... | collective-permute-start | bytes 589832 | tf_op jit(solution)/shard_map/ppermute | solution.py:34
  74.7 6.5 %collective-permute-done.3 = bf16[2,96,1024]{2,1,0:T(8,128)(2,1)S(1)} collective-permute-done((bf16[2,96,1024]{2,1,0:T(8,128)(2,1)S(1)}, bf16[2,96,1024]{2,1,0:T(8,128)(2,1)S(1)}, u32[]{:S(2)}, u32[]{:S(2)}) %collective-permute-start.3) | collective-permute-done | bytes 393248 | tf_op jit(solution)/shard_map/ppermute | solution.py:34
  81.2 1.9 %collective-permute-start.5 = (bf16[96,1024]{1,0:T(8,128)(2,1)S(1)}, bf16[96,1024]{1,0:T(8,128)(2,1)S(1)}, u32[]{:S(2)}, u32[]{:S(2)}) collective-permute-start(bf16[96,1024]{1,0:T(8,128)(2,1)S(1)} %fusion), channel_id=1, source_target_pairs={{0,2},{1,3},{2,4},{3,5},{4,6},{5,7},{6,0},{7,1},{8,14},{9,15},{10,... | collective-permute-start | bytes 589832 | tf_op jit(solution)/shard_map/ppermute | solution.py:34
  83.1 0.0 collective-permute-done.4
  83.1 7.7 %collective-permute-done.5 = bf16[96,1024]{1,0:T(8,128)(2,1)S(1)} collective-permute-done((bf16[96,1024]{1,0:T(8,128)(2,1)S(1)}, bf16[96,1024]{1,0:T(8,128)(2,1)S(1)}, u32[]{:S(2)}, u32[]{:S(2)}) %collective-permute-start.5) | collective-permute-done | bytes 196640 | tf_op jit(solution)/shard_map/ppermute | solution.py:34
  90.9 0.8 fusion.4
  (9 shorter events, 0.3 us)
Async XLA Ops:
  27.9 5.1 %copy-start.4 = (s32[1920]{0:T(1024)S(1)}, s32[1920]{0:T(1024)}, u32[]{:S(2)}) copy-start(s32[1920]{0:T(1024)} %param.8) | copy-start | bytes 23044
  27.9 5.1 %copy-start.3 = (s32[1024]{0:T(1024)S(1)}, s32[1024]{0:T(1024)}, u32[]{:S(2)}) copy-start(s32[1024]{0:T(1024)} %param.9) | copy-start | bytes 12292
  27.9 20.6 %all-to-all-start.1 = ((bf16[8,6,8,1920]{3,2,1,0:T(8,128)(2,1)}), bf16[8,6,8,1920]{3,2,1,0:T(8,128)(2,1)S(1)}, u32[]{:S(2)}, u32[]{:S(2)}) async-start(bf16[8,6,8,1920]{3,2,1,0:T(8,128)(2,1)} %broadcast_in_dim.15), calls=%async_computation.1 | async-start | bytes 2949120 | tf_op jit(solution)/shard_map/all_to_all | solution.py:16
  33.0 2.1 %copy-start = (bf16[1,1920,1024]{2,1,0:T(8,128)(2,1)S(1)}, bf16[1,1920,1024]{2,1,0:T(8,128)(2,1)}, u32[]{:S(2)}) copy-start(bf16[1,1920,1024]{2,1,0:T(8,128)(2,1)} %param.6) | copy-start | bytes 11796484
  36.3 1.9 %copy-start.1 = (bf16[1920,1024]{1,0:T(8,128)(2,1)}, bf16[1920,1024]{1,0:T(8,128)(2,1)S(1)}, u32[]{:S(2)}) copy-start(bf16[1920,1024]{1,0:T(8,128)(2,1)S(1)} %shard_map.55) | copy-start | bytes 11796484
  48.5 6.1 %collective-permute-start = (bf16[8,6,8,1920]{3,2,1,0:T(8,128)(2,1)S(1)}, bf16[8,6,8,1920]{3,2,1,0:T(8,128)(2,1)S(1)}, u32[]{:S(2)}, u32[]{:S(2)}) collective-permute-start(bf16[8,6,8,1920]{3,2,1,0:T(8,128)(2,1)S(1)} %all-to-all-done.1), channel_id=1, source_target_pairs={{0,8},{8,0},{1,9},{9,1},{2,10},{10,2},{3,11},{11,3},{4,12},{12,4},... | collective-permute-start | bytes 4423688 | tf_op jit(solution)/shard_map/ppermute | solution.py:97
  50.5 4.1 %copy-start.2 = (bf16[1920,1024]{1,0:T(8,128)(2,1)S(1)}, bf16[1920,1024]{1,0:T(8,128)(2,1)}, u32[]{:S(2)}) copy-start(bf16[1920,1024]{1,0:T(8,128)(2,1)} %copy-done.1) | copy-start | bytes 11796484
  57.0 9.2 %collective-permute-start.2 = (bf16[96,1024]{1,0:T(8,128)(2,1)S(1)}, bf16[96,1024]{1,0:T(8,128)(2,1)S(1)}, u32[]{:S(2)}, u32[]{:S(2)}) collective-permute-start(bf16[96,1024]{1,0:T(8,128)(2,1)S(1)} %get-tuple-element.22), channel_id=1, source_target_pairs={{0,1},{1,2},{2,3},{3,4},{4,5},{5,6},{6,7},{7,0},{8,15},{9,8},{10,9... | collective-permute-start | bytes 589832 | tf_op jit(solution)/shard_map/ppermute | solution.py:34
  59.7 11.4 %collective-permute-start.1 = (bf16[2,96,1024]{2,1,0:T(8,128)(2,1)S(1)}, bf16[2,96,1024]{2,1,0:T(8,128)(2,1)S(1)}, u32[]{:S(2)}, u32[]{:S(2)}) collective-permute-start(bf16[2,96,1024]{2,1,0:T(8,128)(2,1)S(1)} %pad_maximum_fusion.1), channel_id=1, source_target_pairs={{0,7},{1,0},{2,1},{3,2},{4,3},{5,4},{6,5},{7,6},{8,9},{9,10},{10,1... | collective-permute-start | bytes 1179656 | tf_op jit(solution)/shard_map/ppermute | solution.py:34
  66.3 14.8 %collective-permute-start.3 = (bf16[2,96,1024]{2,1,0:T(8,128)(2,1)S(1)}, bf16[2,96,1024]{2,1,0:T(8,128)(2,1)S(1)}, u32[]{:S(2)}, u32[]{:S(2)}) collective-permute-start(bf16[2,96,1024]{2,1,0:T(8,128)(2,1)S(1)} %pad_maximum_fusion.2), channel_id=1, source_target_pairs={{0,1},{1,2},{2,3},{3,4},{4,5},{5,6},{6,7},{7,0},{8,15},{9,8},{10,9... | collective-permute-start | bytes 1179656 | tf_op jit(solution)/shard_map/ppermute | solution.py:34
  71.1 12.0 %collective-permute-start.4 = (bf16[96,1024]{1,0:T(8,128)(2,1)S(1)}, bf16[96,1024]{1,0:T(8,128)(2,1)S(1)}, u32[]{:S(2)}, u32[]{:S(2)}) collective-permute-start(bf16[96,1024]{1,0:T(8,128)(2,1)S(1)} %fusion.1), channel_id=1, source_target_pairs={{0,6},{1,7},{2,0},{3,1},{4,2},{5,3},{6,4},{7,5},{8,10},{9,11},{10,... | collective-permute-start | bytes 589832 | tf_op jit(solution)/shard_map/ppermute | solution.py:34
  81.2 9.7 %collective-permute-start.5 = (bf16[96,1024]{1,0:T(8,128)(2,1)S(1)}, bf16[96,1024]{1,0:T(8,128)(2,1)S(1)}, u32[]{:S(2)}, u32[]{:S(2)}) collective-permute-start(bf16[96,1024]{1,0:T(8,128)(2,1)S(1)} %fusion), channel_id=1, source_target_pairs={{0,2},{1,3},{2,4},{3,5},{4,6},{5,7},{6,0},{7,1},{8,14},{9,15},{10,... | collective-permute-start | bytes 589832 | tf_op jit(solution)/shard_map/ppermute | solution.py:34

commit v5 on v4

--- a/solution.py
+++ b/solution.py
@@ -74,7 +74,7 @@
     depth, width = weights.shape
     return pl.pallas_call(
         mask_rows,
-        out_shape=jax.ShapeDtypeStruct(weights.shape, weights.dtype),
+        out_shape=pltpu.VMEM(weights.shape, weights.dtype),
         grid=(steps,),
         in_specs=[
             pl.BlockSpec(memory_space=pltpu.SMEM),

time: 92.2 us -> 92.2 us (level)
  no operation moved by 1% of the time
where the time goes in v5:
time: 92.2 us; the launch traced here: 91.7 us
  waiting for transfers between devices  29.4 us (32%)
  blocking collectives  25.8 us (28%)
  starting transfers between devices  20.8 us (23%)
  local copies, waits for them, and re-layouts  6.35 us (7%)
  matrix products  5.91 us (6%)
  other arithmetic  1.24 us (1%)
  Pallas kernels  1.19 us (1%)
  between operations  0.99 us (1%)
    all_to_all x1, blocking collectives, gather_z(): lax.all_to_all(copies, 'zh', 0, 0, tiled=False, axis_index_groups=[ORDER])  25.8 us
    ppermute x5, waiting for transfers between devices, mirrored(): return lax.ppermute(array, ('c', 'y'), pairs)  19.1 us
    ppermute x5, starting transfers between devices, mirrored(): return lax.ppermute(array, ('c', 'y'), pairs)  14.4 us
    all_to_all x1, waiting for transfers between devices, gather(): return lax.all_to_all(copies, axis, 0, 0, tiled=False)  10.3 us
    dot_general x2, matrix products, product(): jnp.dot(rows.reshape(-1, rows.shape[-1]), masked, preferred_element_type=...  5.91 us
    all_to_all x1, starting transfers between devices, gather(): return lax.all_to_all(copies, axis, 0, 0, tiled=False)  4.43 us
    unnamed x10, local copies, waits for them, and re-layouts  3.97 us
    ppermute x1, starting transfers between devices, on_device(): theirs = lax.ppermute(mine, 'c', [(0, 1), (1, 0)])  1.91 us
  transfers between devices with their start and end apart: 7, of which 5 were waited for; matrix products, arithmetic and copies ran while one was open for 5% of the time, Pallas kernels for 1%

profile of v5, /device:TPU:32, one launch (start us, length us, event | category | flops | bytes accessed | tf_op | source)
XLA Modules:
  0.0 91.7 jit_solution(10922039075052367928)
XLA Ops:
  0.0 0.8 broadcast_in_dim.14
  0.8 25.8 %all_to_all.10 = bf16[6,8,1920]{2,1,0:T(8,128)(2,1)S(1)} all-to-all(bf16[6,8,1920]{2,1,0:T(8,128)(2,1)S(1)} %broadcast_in_dim.14), channel_id=1, replica_groups={{640,512,0,128,256,384},{641,513,1,129,257,385},{642,514,2,130,258,386}..., dimensions={0} | all-to-all | bytes 368640 | tf_op jit(solution)/shard_map/all_to_all | solution.py:24
  26.7 1.2 %broadcast_in_dim.15 = bf16[8,6,8,1920]{3,2,1,0:T(8,128)(2,1)} broadcast(bf16[6,8,1920]{2,1,0:T(8,128)(2,1)S(1)} %pad_maximum_fusion.3), dimensions={1,2,3} | broadcast | bytes 1658880 | tf_op jit(solution)/shard_map/broadcast_in_dim | solution.py:15
  27.9 0.0 copy-start.4
  27.9 0.0 copy-start.3
  27.9 4.4 %all-to-all-start.1 = ((bf16[8,6,8,1920]{3,2,1,0:T(8,128)(2,1)}), bf16[8,6,8,1920]{3,2,1,0:T(8,128)(2,1)S(1)}, u32[]{:S(2)}, u32[]{:S(2)}) async-start(bf16[8,6,8,1920]{3,2,1,0:T(8,128)(2,1)} %broadcast_in_dim.15), calls=%async_computation.1 | async-start | bytes 2949120 | tf_op jit(solution)/shard_map/all_to_all | solution.py:16
  33.0 0.0 copy-done.4
  33.0 0.0 copy-done.3
  33.0 0.0 copy-start
  33.0 2.1 %copy-done = bf16[1,1920,1024]{2,1,0:T(8,128)(2,1)S(1)} copy-done((bf16[1,1920,1024]{2,1,0:T(8,128)(2,1)S(1)}, bf16[1,1920,1024]{2,1,0:T(8,128)(2,1)}, u32[]{:S(2)}) %copy-start) | copy-done | bytes 3932184
  35.1 1.2 %shard_map.55 = bf16[1920,1024]{1,0:T(8,128)(2,1)S(1)} custom-call(s32[1]{0:T(128)S(6)} %copy.10.occ_ref, s32[5,3,128]{2,1,0:T(4,128)S(1)} %reshape.34.vir_ref, s32[8,128]{1,0:T(8,128)S(1)} %bitcast.62, bf16[1920,1024]{1,0:T(8,128)(2,1)S(1)} %bitcast.61), custom_call_target="tpu_custom_call" | custom-call | flops 1966080 | bytes 7864320 | tf_op jit(solution)/shard_map/pallas_call | solution.py:75
  36.3 0.0 copy-start.1
  36.3 1.9 %copy-done.1 = bf16[1920,1024]{1,0:T(8,128)(2,1)} copy-done((bf16[1920,1024]{1,0:T(8,128)(2,1)}, bf16[1920,1024]{1,0:T(8,128)(2,1)S(1)}, u32[]{:S(2)}) %copy-start.1) | copy-done | bytes 3932184
  38.2 10.3 %all-to-all-done.1 = bf16[8,6,8,1920]{3,2,1,0:T(8,128)(2,1)S(1)} async-done(((bf16[8,6,8,1920]{3,2,1,0:T(8,128)(2,1)}), bf16[8,6,8,1920]{3,2,1,0:T(8,128)(2,1)S(1)}, u32[]{:S(2)}, u32[]{:S(2)}) %all-to-all-start.1) | async-done | bytes 1474592 | tf_op jit(solution)/shard_map/all_to_all | solution.py:16
  48.5 1.9 %collective-permute-start = (bf16[8,6,8,1920]{3,2,1,0:T(8,128)(2,1)S(1)}, bf16[8,6,8,1920]{3,2,1,0:T(8,128)(2,1)S(1)}, u32[]{:S(2)}, u32[]{:S(2)}) collective-permute-start(bf16[8,6,8,1920]{3,2,1,0:T(8,128)(2,1)S(1)} %all-to-all-done.1), channel_id=1, source_target_pairs={{0,8},{8,0},{1,9},{9,1},{2,10},{10,2},{3,11},{11,3},{4,12},{12,4},... | collective-permute-start | bytes 4423688 | tf_op jit(solution)/shard_map/ppermute | solution.py:97
  50.5 0.0 copy-start.2
  50.6 4.0 %convolution_convert_fusion.1 = bf16[384,1024]{1,0:T(8,128)(2,1)S(1)} fusion(bf16[384,1920]{1,0:T(8,128)(2,1)S(1)} %bitcast.64, bf16[1920,1024]{1,0:T(8,128)(2,1)} %copy-done.1), kind=kOutput, calls=%fused_computation.2 | convolution fusion | flops 1510342656 | bytes 6193152 | tf_op jit(solution)/shard_map/dot_general | solution.py:100
  54.6 0.0 collective-permute-done
  54.6 0.0 copy-done.2
  54.6 1.9 %broadcast_select_fusion.1 = (bf16[384,1024]{1,0:T(8,128)(2,1)S(1)}, bf16[384,1024]{1,0:T(8,128)(2,1)S(1)}) fusion(bf16[384,1024]{1,0:T(8,128)(2,1)S(1)} %convolution_convert_fusion.1, pred[]{:T(512)S(6)} %eq.13, bf16[384,1920]{1,0:T(8,128)(2,1)S(1)} %bitcast.71, bf16[1920,1024]{1,0:T(8,128)(2,1)S(1)} %copy-done.2), kind=kOutput, calls=%fused_computation.6 | convolution fusion | flops 1511129088 | bytes 7766017 | tf_op jit(solution)/shard_map/dot_general | solution.py:100
  56.5 0.2 copy_bitcast_fusion
  56.7 0.1 pad_maximum_fusion
  56.8 0.2 dynamic-slice_bitcast_fusion
  57.0 2.6 %collective-permute-start.2 = (bf16[96,1024]{1,0:T(8,128)(2,1)S(1)}, bf16[96,1024]{1,0:T(8,128)(2,1)S(1)}, u32[]{:S(2)}, u32[]{:S(2)}) collective-permute-start(bf16[96,1024]{1,0:T(8,128)(2,1)S(1)} %get-tuple-element.22), channel_id=1, source_target_pairs={{0,1},{1,2},{2,3},{3,4},{4,5},{5,6},{6,7},{7,0},{8,15},{9,8},{10,9... | collective-permute-start | bytes 589832 | tf_op jit(solution)/shard_map/ppermute | solution.py:34
  59.7 4.5 %collective-permute-start.1 = (bf16[2,96,1024]{2,1,0:T(8,128)(2,1)S(1)}, bf16[2,96,1024]{2,1,0:T(8,128)(2,1)S(1)}, u32[]{:S(2)}, u32[]{:S(2)}) collective-permute-start(bf16[2,96,1024]{2,1,0:T(8,128)(2,1)S(1)} %pad_maximum_fusion.1), channel_id=1, source_target_pairs={{0,7},{1,0},{2,1},{3,2},{4,3},{5,4},{6,5},{7,6},{8,9},{9,10},{10,1... | collective-permute-start | bytes 1179656 | tf_op jit(solution)/shard_map/ppermute | solution.py:34
  64.1 2.0 %collective-permute-done.2 = bf16[96,1024]{1,0:T(8,128)(2,1)S(1)} collective-permute-done((bf16[96,1024]{1,0:T(8,128)(2,1)S(1)}, bf16[96,1024]{1,0:T(8,128)(2,1)S(1)}, u32[]{:S(2)}, u32[]{:S(2)}) %collective-permute-start.2) | collective-permute-done | bytes 196640 | tf_op jit(solution)/shard_map/ppermute | solution.py:34
  66.3 1.9 %collective-permute-start.3 = (bf16[2,96,1024]{2,1,0:T(8,128)(2,1)S(1)}, bf16[2,96,1024]{2,1,0:T(8,128)(2,1)S(1)}, u32[]{:S(2)}, u32[]{:S(2)}) collective-permute-start(bf16[2,96,1024]{2,1,0:T(8,128)(2,1)S(1)} %pad_maximum_fusion.2), channel_id=1, source_target_pairs={{0,1},{1,2},{2,3},{3,4},{4,5},{5,6},{6,7},{7,0},{8,15},{9,8},{10,9... | collective-permute-start | bytes 1179656 | tf_op jit(solution)/shard_map/ppermute | solution.py:34
  68.2 2.9 %collective-permute-done.1 = bf16[2,96,1024]{2,1,0:T(8,128)(2,1)S(1)} collective-permute-done((bf16[2,96,1024]{2,1,0:T(8,128)(2,1)S(1)}, bf16[2,96,1024]{2,1,0:T(8,128)(2,1)S(1)}, u32[]{:S(2)}, u32[]{:S(2)}) %collective-permute-start.1) | collective-permute-done | bytes 393248 | tf_op jit(solution)/shard_map/ppermute | solution.py:34
  71.1 3.6 %collective-permute-start.4 = (bf16[96,1024]{1,0:T(8,128)(2,1)S(1)}, bf16[96,1024]{1,0:T(8,128)(2,1)S(1)}, u32[]{:S(2)}, u32[]{:S(2)}) collective-permute-start(bf16[96,1024]{1,0:T(8,128)(2,1)S(1)} %fusion.1), channel_id=1, source_target_pairs={{0,6},{1,7},{2,0},{3,1},{4,2},{5,3},{6,4},{7,5},{8,10},{9,11},{10,... | collective-permute-start | bytes 589832 | tf_op jit(solution)/shard_map/ppermute | solution.py:34
  74.7 6.5 %collective-permute-done.3 = bf16[2,96,1024]{2,1,0:T(8,128)(2,1)S(1)} collective-permute-done((bf16[2,96,1024]{2,1,0:T(8,128)(2,1)S(1)}, bf16[2,96,1024]{2,1,0:T(8,128)(2,1)S(1)}, u32[]{:S(2)}, u32[]{:S(2)}) %collective-permute-start.3) | collective-permute-done | bytes 393248 | tf_op jit(solution)/shard_map/ppermute | solution.py:34
  81.2 1.9 %collective-permute-start.5 = (bf16[96,1024]{1,0:T(8,128)(2,1)S(1)}, bf16[96,1024]{1,0:T(8,128)(2,1)S(1)}, u32[]{:S(2)}, u32[]{:S(2)}) collective-permute-start(bf16[96,1024]{1,0:T(8,128)(2,1)S(1)} %fusion), channel_id=1, source_target_pairs={{0,2},{1,3},{2,4},{3,5},{4,6},{5,7},{6,0},{7,1},{8,14},{9,15},{10,... | collective-permute-start | bytes 589832 | tf_op jit(solution)/shard_map/ppermute | solution.py:34
  83.1 0.0 collective-permute-done.4
  83.1 7.7 %collective-permute-done.5 = bf16[96,1024]{1,0:T(8,128)(2,1)S(1)} collective-permute-done((bf16[96,1024]{1,0:T(8,128)(2,1)S(1)}, bf16[96,1024]{1,0:T(8,128)(2,1)S(1)}, u32[]{:S(2)}, u32[]{:S(2)}) %collective-permute-start.5) | collective-permute-done | bytes 196640 | tf_op jit(solution)/shard_map/ppermute | solution.py:34
  90.9 0.8 fusion.4
  (9 shorter events, 0.3 us)
Async XLA Ops:
  27.9 5.1 %copy-start.4 = (s32[1920]{0:T(1024)S(1)}, s32[1920]{0:T(1024)}, u32[]{:S(2)}) copy-start(s32[1920]{0:T(1024)} %param.8) | copy-start | bytes 23044
  27.9 5.1 %copy-start.3 = (s32[1024]{0:T(1024)S(1)}, s32[1024]{0:T(1024)}, u32[]{:S(2)}) copy-start(s32[1024]{0:T(1024)} %param.9) | copy-start | bytes 12292
  27.9 20.6 %all-to-all-start.1 = ((bf16[8,6,8,1920]{3,2,1,0:T(8,128)(2,1)}), bf16[8,6,8,1920]{3,2,1,0:T(8,128)(2,1)S(1)}, u32[]{:S(2)}, u32[]{:S(2)}) async-start(bf16[8,6,8,1920]{3,2,1,0:T(8,128)(2,1)} %broadcast_in_dim.15), calls=%async_computation.1 | async-start | bytes 2949120 | tf_op jit(solution)/shard_map/all_to_all | solution.py:16
  33.0 2.1 %copy-start = (bf16[1,1920,1024]{2,1,0:T(8,128)(2,1)S(1)}, bf16[1,1920,1024]{2,1,0:T(8,128)(2,1)}, u32[]{:S(2)}) copy-start(bf16[1,1920,1024]{2,1,0:T(8,128)(2,1)} %param.6) | copy-start | bytes 11796484
  36.3 1.9 %copy-start.1 = (bf16[1920,1024]{1,0:T(8,128)(2,1)}, bf16[1920,1024]{1,0:T(8,128)(2,1)S(1)}, u32[]{:S(2)}) copy-start(bf16[1920,1024]{1,0:T(8,128)(2,1)S(1)} %shard_map.55) | copy-start | bytes 11796484
  48.5 6.1 %collective-permute-start = (bf16[8,6,8,1920]{3,2,1,0:T(8,128)(2,1)S(1)}, bf16[8,6,8,1920]{3,2,1,0:T(8,128)(2,1)S(1)}, u32[]{:S(2)}, u32[]{:S(2)}) collective-permute-start(bf16[8,6,8,1920]{3,2,1,0:T(8,128)(2,1)S(1)} %all-to-all-done.1), channel_id=1, source_target_pairs={{0,8},{8,0},{1,9},{9,1},{2,10},{10,2},{3,11},{11,3},{4,12},{12,4},... | collective-permute-start | bytes 4423688 | tf_op jit(solution)/shard_map/ppermute | solution.py:97
  50.5 4.1 %copy-start.2 = (bf16[1920,1024]{1,0:T(8,128)(2,1)S(1)}, bf16[1920,1024]{1,0:T(8,128)(2,1)}, u32[]{:S(2)}) copy-start(bf16[1920,1024]{1,0:T(8,128)(2,1)} %copy-done.1) | copy-start | bytes 11796484
  57.0 9.2 %collective-permute-start.2 = (bf16[96,1024]{1,0:T(8,128)(2,1)S(1)}, bf16[96,1024]{1,0:T(8,128)(2,1)S(1)}, u32[]{:S(2)}, u32[]{:S(2)}) collective-permute-start(bf16[96,1024]{1,0:T(8,128)(2,1)S(1)} %get-tuple-element.22), channel_id=1, source_target_pairs={{0,1},{1,2},{2,3},{3,4},{4,5},{5,6},{6,7},{7,0},{8,15},{9,8},{10,9... | collective-permute-start | bytes 589832 | tf_op jit(solution)/shard_map/ppermute | solution.py:34
  59.7 11.4 %collective-permute-start.1 = (bf16[2,96,1024]{2,1,0:T(8,128)(2,1)S(1)}, bf16[2,96,1024]{2,1,0:T(8,128)(2,1)S(1)}, u32[]{:S(2)}, u32[]{:S(2)}) collective-permute-start(bf16[2,96,1024]{2,1,0:T(8,128)(2,1)S(1)} %pad_maximum_fusion.1), channel_id=1, source_target_pairs={{0,7},{1,0},{2,1},{3,2},{4,3},{5,4},{6,5},{7,6},{8,9},{9,10},{10,1... | collective-permute-start | bytes 1179656 | tf_op jit(solution)/shard_map/ppermute | solution.py:34
  66.3 14.8 %collective-permute-start.3 = (bf16[2,96,1024]{2,1,0:T(8,128)(2,1)S(1)}, bf16[2,96,1024]{2,1,0:T(8,128)(2,1)S(1)}, u32[]{:S(2)}, u32[]{:S(2)}) collective-permute-start(bf16[2,96,1024]{2,1,0:T(8,128)(2,1)S(1)} %pad_maximum_fusion.2), channel_id=1, source_target_pairs={{0,1},{1,2},{2,3},{3,4},{4,5},{5,6},{6,7},{7,0},{8,15},{9,8},{10,9... | collective-permute-start | bytes 1179656 | tf_op jit(solution)/shard_map/ppermute | solution.py:34
  71.1 12.0 %collective-permute-start.4 = (bf16[96,1024]{1,0:T(8,128)(2,1)S(1)}, bf16[96,1024]{1,0:T(8,128)(2,1)S(1)}, u32[]{:S(2)}, u32[]{:S(2)}) collective-permute-start(bf16[96,1024]{1,0:T(8,128)(2,1)S(1)} %fusion.1), channel_id=1, source_target_pairs={{0,6},{1,7},{2,0},{3,1},{4,2},{5,3},{6,4},{7,5},{8,10},{9,11},{10,... | collective-permute-start | bytes 589832 | tf_op jit(solution)/shard_map/ppermute | solution.py:34
  81.2 9.7 %collective-permute-start.5 = (bf16[96,1024]{1,0:T(8,128)(2,1)S(1)}, bf16[96,1024]{1,0:T(8,128)(2,1)S(1)}, u32[]{:S(2)}, u32[]{:S(2)}) collective-permute-start(bf16[96,1024]{1,0:T(8,128)(2,1)S(1)} %fusion), channel_id=1, source_target_pairs={{0,2},{1,3},{2,4},{3,5},{4,6},{5,7},{6,0},{7,1},{8,14},{9,15},{10,... | collective-permute-start | bytes 589832 | tf_op jit(solution)/shard_map/ppermute | solution.py:34
